TPU v7x, 128 devices: a whole 4x4x4 slice. The times are simulated.
128 devices in a mesh: wide: 32 (over x, y, core), narrow: 4 (over z).
Axes of the slice: x: 4, y: 4, z: 4, core: 2. Of those that a mesh axis runs over, the one named last changes fastest.
Arguments:
- phases: float32 [4, 1024, 128, 128], P(None, 'wide', 'narrow'), may hold values from 0 to 1
- potentials: float32 [2, 1024, 128, 128], P(None, 'wide', 'narrow'), may hold values from -1.5 to 1.5
- leaving: int32 [32, 4], P('wide', 'narrow'), may hold values from 0 to 3
- arriving: int32 [32, 4], P('wide', 'narrow'), may hold values from 0 to 31, as said below
- conc: float32 [4, 2], replicated, may hold values from -1 to 1
- latent: float32 [4], replicated, may hold values from -0.6 to 0.6
Outputs:
- phases_out: float32 [4, 1024, 128, 128], P(None, 'wide', 'narrow')
- potentials_out: float32 [2, 1024, 128, 128], P(None, 'wide', 'narrow')
Inputs may be any that keep to these rules, and one draw needn't show every extreme that they name: In each block row, arriving is a permutation of the block columns, and each entry lies at most 2 columns away from its own column, cyclically; some entry lies exactly 2 away.
All inputs are finite; a program needn't handle non-finite values.
Results may differ from a plain program's by a relative error of at most 0.00012.
Values sent between devices are 32-bit elements; how exact they have to be, the bound alone decides.
A program may use at most 128 MiB of HBM per device.

v0:
```python
import jax
import jax.numpy as jnp
from jax import lax
from jax.sharding import PartitionSpec as P

STEPS = 3
REACH = 2


surface_weight = 1.0
drive_weight = 2.0
time_step = 0.1
diffusion = 1.0


def passed_along(block, axis, distance):
    devices = range(lax.axis_size(axis))
    route = [((i - distance) % len(devices), i) for i in devices]
    return lax.ppermute(block, axis, route)


def extended_2(block, sides, width):
    for axis, dim in sides:
        count = lax.axis_size(axis)
        forward = [(i, i + 1) for i in range(count - 1)]
        forward.append((count - 1, 0))
        backward = [(target, source) for source, target in forward]
        low = lax.ppermute(
            lax.slice_in_dim(block, block.shape[dim] - width, None, axis=dim), axis, forward
        )
        high = lax.ppermute(lax.slice_in_dim(block, 0, width, axis=dim), axis, backward)
        block = jnp.concatenate([low, block, high], axis=dim)
    return block


def update(phase, potent, lap_phase, lap_potent, conc, latent, theta):
    well = phase * (1.0 - phase) * (1.0 - 2.0 * phase)
    slope = 6.0 * phase * (1.0 - phase)
    drive = (
        conc[:, 0, None, None, None] * potent[0]
        + conc[:, 1, None, None, None] * potent[1]
        + latent[:, None, None, None] * theta
    )
    rate = surface_weight * (lap_phase - 18.0 * well) - drive_weight * slope * drive
    rate = rate - jnp.mean(rate, axis=0, keepdims=True)
    new_phase = phase + time_step * rate
    change = new_phase - phase
    source = jnp.stack(
        [
            jnp.sum(conc[:, 0, None, None, None] * change, 0),
            jnp.sum(conc[:, 1, None, None, None] * change, 0),
        ]
    )
    new_potent = potent + time_step * diffusion * lap_potent - source
    return (new_phase, new_potent)


def advance(extended, conc, latent, theta):
    center = extended[:, 1:-1, 1:-1]
    zp = jnp.concatenate([center[..., 1:], center[..., -1:]], -1)
    zm = jnp.concatenate([center[..., :1], center[..., :-1]], -1)
    lapped = (
        extended[:, 2:, 1:-1]
        + extended[:, :-2, 1:-1]
        + extended[:, 1:-1, 2:]
        + extended[:, 1:-1, :-2]
        + zp
        + zm
        - 6.0 * center
    )
    new_phase, new_potent = update(
        center[:4], center[4:], lapped[:4], lapped[4:], conc, latent, theta
    )
    return jnp.concatenate([new_phase, new_potent], 0)


def shards(phases, potentials, leaving, arriving, conc, latent):
    fields = jnp.concatenate([phases, potentials], 0)
    edge = phases.shape[1]
    depth = fields.shape[3]
    slot = leaving[0, 0]
    source = arriving[0, 0]
    block = lax.dynamic_slice_in_dim(fields, slot * edge, edge, 3)
    packed = block.reshape(1, 6, edge, edge * edge)
    columns = lax.axis_size("wide")
    here = lax.axis_index("wide")
    needed = (here - source) % columns
    offset = jnp.where(needed > columns // 2, needed - columns, needed)
    arrived = packed[0]
    for distance in range(-REACH, REACH + 1):
        if distance != 0:
            received = passed_along(packed, "wide", distance)
            arrived = jnp.where(offset == distance, received[0], arrived)
    fields = lax.dynamic_update_slice_in_dim(
        fields, arrived.reshape(6, edge, edge, edge), slot * edge, 3
    )
    theta = 4.0 * (jnp.arange(depth).astype(jnp.float32) + 0.5) / depth - 2.0
    for step in range(STEPS):
        extended = extended_2(fields, (("wide", 1), ("narrow", 2)), 1)
        fields = advance(extended, conc, latent, theta)
    return (fields[:4], fields[4:])


def solution(mesh):
    in_specs = (
        P(None, "wide", "narrow", None),
        P(None, "wide", "narrow", None),
        P("wide", "narrow"),
        P("wide", "narrow"),
        P(),
        P(),
    )
    out_specs = (P(None, "wide", "narrow", None), P(None, "wide", "narrow", None))
    return jax.shard_map(shards, mesh=mesh, in_specs=in_specs, out_specs=out_specs, check_vma=False)
```

profile of v0, /device:TPU:0, one launch (start us, length us, event | category | flops | bytes accessed | tf_op | source)
XLA Modules:
  0.0 176.4 jit_solution(16017507314842753161)
XLA Ops:
  4.4 2.5 %constant_dynamic-slice_fusion = f32[6,32,32,32]{3,2,1,0:T(8,128)} fusion(f32[6,32,32,128]{3,2,1,0:T(8,128)S(1)} %constant_dynamic-update-slice_fusion, s32[]{:T(128)S(6)} %select_n.47), kind=kLoop, calls=%fused_computation.160 | loop fusion | bytes 1572868 | tf_op jit(solution)/shard_map/dynamic_slice | solution.py:83
  6.9 3.7 %reshape.64 = f32[1,6,32,1024]{3,2,1,0:T(8,128)} reshape(f32[6,32,32,32]{3,2,1,0:T(8,128)} %constant_dynamic-slice_fusion) | data formatting | bytes 1572864 | tf_op jit(solution)/shard_map/reshape | solution.py:84
  12.2 5.1 %collective-permute-start.2 = (f32[1,6,32,1024]{3,2,1,0:T(8,128)}, f32[1,6,32,1024]{3,2,1,0:T(8,128)}, u32[]{:S(2)}, u32[]{:S(2)}) collective-permute-start(f32[1,6,32,1024]{3,2,1,0:T(8,128)} %reshape.64), channel_id=1, source_target_pairs={{4,0},{8,4},{12,8},{16,12},{20,16},{24,20},{28,24},{32,28},{36,32}... | collective-permute-start | bytes 2359304 | tf_op jit(solution)/shard_map/ppermute | solution.py:19
  18.4 16.1 %collective-permute-done = f32[1,6,32,1024]{3,2,1,0:T(8,128)} collective-permute-done((f32[1,6,32,1024]{3,2,1,0:T(8,128)}, f32[1,6,32,1024]{3,2,1,0:T(8,128)}, u32[]{:S(2)}, u32[]{:S(2)}) %collective-permute-start) | collective-permute-done | bytes 786464 | tf_op jit(solution)/shard_map/ppermute | solution.py:19
  34.6 3.2 %squeeze.17 = f32[6,32,32,32]{3,2,1,0:T(8,128)} reshape(f32[1,6,32,1024]{3,2,1,0:T(8,128)} %collective-permute-done) | data formatting | bytes 1572864 | tf_op jit(solution)/shard_map/squeeze | solution.py:93
  37.8 4.3 %collective-permute-done.1 = f32[1,6,32,1024]{3,2,1,0:T(8,128)} collective-permute-done((f32[1,6,32,1024]{3,2,1,0:T(8,128)}, f32[1,6,32,1024]{3,2,1,0:T(8,128)}, u32[]{:S(2)}, u32[]{:S(2)}) %collective-permute-start.1) | collective-permute-done | bytes 786464 | tf_op jit(solution)/shard_map/ppermute | solution.py:19
  42.1 3.2 %squeeze.18 = f32[6,32,32,32]{3,2,1,0:T(8,128)} reshape(f32[1,6,32,1024]{3,2,1,0:T(8,128)} %collective-permute-done.1) | data formatting | bytes 1572864 | tf_op jit(solution)/shard_map/squeeze | solution.py:93
  45.4 3.3 %squeeze.19 = f32[6,32,32,32]{3,2,1,0:T(8,128)} reshape(f32[1,6,32,1024]{3,2,1,0:T(8,128)} %collective-permute-done.2) | data formatting | bytes 1572864 | tf_op jit(solution)/shard_map/squeeze | solution.py:93
  48.7 3.2 %squeeze.20 = f32[6,32,32,32]{3,2,1,0:T(8,128)} reshape(f32[1,6,32,1024]{3,2,1,0:T(8,128)} %collective-permute-done.3) | data formatting | bytes 1572864 | tf_op jit(solution)/shard_map/squeeze | solution.py:93
  51.9 5.4 %select_select_fusion = f32[6,32,32,32]{3,2,1,0:T(8,128)} fusion(f32[6,32,32,32]{3,2,1,0:T(8,128)} %squeeze.17, f32[6,32,32,32]{3,2,1,0:T(8,128)} %squeeze.18, f32[6,32,32,32]{3,2,1,0:T(8,128)} %squeeze.19, f32[6,32,32,32]{3,2,1,0:T(8,128)} %squeeze.20, pred[]{:T(512)S(6)} %eq.17, pred[]{:T(512)S(6)} %eq.16, pred[]{:T(512)S(6)} %eq.15, pred[]{:T(512)S(6)} %eq.14, ...), kind=kLoop, calls=%fused_computation.86 | loop fusion | flops 786432 | bytes 4718600 | tf_op jit(solution)/shard_map/jit(_where)/select_n | solution.py:93
  57.3 15.0 %dynamic_update_slice.3 = f32[6,32,32,128]{3,2,1,0:T(8,128)S(1)} dynamic-update-slice(f32[6,32,32,128]{3,2,1,0:T(8,128)S(1)} %constant_dynamic-update-slice_fusion, f32[6,32,32,32]{3,2,1,0:T(8,128)} %select_select_fusion, s32[]{:T(128)} %constant.17.clone.1, s32[]{:T(128)} %constant.17.clone.1, s32[]{:T(128)} %constant.17.clone.1, s32[]{:T(128)S(6)} %select_n.47) | dynamic-update-slice | bytes 1572868 | tf_op jit(solution)/shard_map/dynamic_update_slice | solution.py:94
  75.8 5.2 %collective-permute-done.5 = f32[6,1,32,128]{3,2,1,0:T(8,128)S(1)} collective-permute-done((f32[6,1,32,128]{3,2,1,0:T(8,128)S(1)}, f32[6,1,32,128]{3,2,1,0:T(8,128)S(1)}, u32[]{:S(2)}, u32[]{:S(2)}) %collective-permute-start.5) | collective-permute-done | bytes 98336 | tf_op jit(solution)/shard_map/ppermute | solution.py:28
  81.2 24.6 %collective-permute-start.6 = (f32[6,34,1,128]{3,1,2,0:T(8,128)S(1)}, f32[6,34,1,128]{3,1,2,0:T(8,128)S(1)}, u32[]{:S(2)}, u32[]{:S(2)}) collective-permute-start(f32[6,34,1,128]{3,1,2,0:T(8,128)S(1)} %copy.12), channel_id=1, source_target_pairs={{1,0},{2,1},{3,2},{0,3},{5,4},{6,5},{7,6},{4,7},{9,8},{10,9},{11,1... | collective-permute-start | bytes 313352 | tf_op jit(solution)/shard_map/ppermute | solution.py:31
  108.4 3.8 %collective-permute-done.7 = f32[6,34,1,128]{3,1,2,0:T(8,128)S(1)} collective-permute-done((f32[6,34,1,128]{3,1,2,0:T(8,128)S(1)}, f32[6,34,1,128]{3,1,2,0:T(8,128)S(1)}, u32[]{:S(2)}, u32[]{:S(2)}) %collective-permute-start.7) | collective-permute-done | bytes 104480 | tf_op jit(solution)/shard_map/ppermute | solution.py:28
  112.4 3.7 %fusion.25 = f32[6,32,32,128]{3,2,1,0:T(8,128)S(1)} fusion(f32[6,34,1,128]{3,2,1,0:T(1,128)S(1)} %copy.15, f32[6,1,32,128]{3,2,1,0:T(8,128)S(1)} %collective-permute-done.4, f32[6,32,32,128]{3,2,1,0:T(8,128)S(1)} %dynamic_update_slice.3, f32[6,1,32,128]{3,2,1,0:T(8,128)S(1)} %collective-permute-done.5, f32[6,34,1,128]{3,2,1,0:T(1,128)S(1)} %copy.13, ...), kind=kLoop, calls=%fused_computation.76 | loop fusion | flops 13369344 | bytes 12988416 | tf_op jit(solution)/shard_map/sub | solution.py:63
  118.5 3.8 %fusion.7 = (f32[6,32,32,127]{3,2,1,0:T(8,128)}, f32[6,32,32,127]{3,2,1,0:T(8,128)}) fusion(f32[4,32,32,128]{3,2,1,0:T(8,128)S(1)} %get-tuple-element.16, f32[2,32,32,128]{3,2,1,0:T(8,128)S(1)} %fusion.51), kind=kLoop, calls=%fused_computation.33 | loop fusion | flops 1560576 | bytes 9388032 | tf_op jit(solution)/shard_map/concatenate | solution.py:74
  122.9 3.7 %fusion.6 = (f32[6,32,32,1]{3,2,1,0:T(8,128)}, f32[6,32,32,1]{3,2,1,0:T(8,128)}) fusion(f32[4,32,32,128]{3,2,1,0:T(8,128)S(1)} %get-tuple-element.16, f32[2,32,32,128]{3,2,1,0:T(8,128)S(1)} %fusion.51), kind=kLoop, calls=%fused_computation.32 | loop fusion | flops 12288 | bytes 3194880 | tf_op jit(solution)/shard_map/concatenate | solution.py:74
  126.6 3.2 %collective-permute-done.9 = f32[6,1,32,128]{3,2,1,0:T(8,128)S(1)} collective-permute-done((f32[6,1,32,128]{3,2,1,0:T(8,128)S(1)}, f32[6,1,32,128]{3,2,1,0:T(8,128)S(1)}, u32[]{:S(2)}, u32[]{:S(2)}) %collective-permute-start.9) | collective-permute-done | bytes 98336 | tf_op jit(solution)/shard_map/ppermute | solution.py:28
  132.5 2.4 %collective-permute-done.10 = f32[6,34,1,128]{3,1,2,0:T(8,128)S(1)} collective-permute-done((f32[6,34,1,128]{3,1,2,0:T(8,128)S(1)}, f32[6,34,1,128]{3,1,2,0:T(8,128)S(1)}, u32[]{:S(2)}, u32[]{:S(2)}) %collective-permute-start.10) | collective-permute-done | bytes 104480 | tf_op jit(solution)/shard_map/ppermute | solution.py:31
  136.6 7.9 %fusion.11 = f32[6,32,32,128]{3,2,1,0:T(8,128)S(1)} fusion(f32[2,32,32,128]{3,2,1,0:T(8,128)S(1)} %fusion.51, f32[4,32,32,128]{3,2,1,0:T(8,128)S(1)} %get-tuple-element.16, f32[6,34,1,128]{3,2,1,0:T(1,128)S(1)} %copy.19, f32[6,1,32,128]{3,2,1,0:T(8,128)S(1)} %collective-permute-done.8, f32[6,1,32,128]{3,2,1,0:T(8,128)S(1)} %collective-permute-done.9, ...), kind=kLoop, calls=%fused_computation.37 | loop fusion | flops 17301504 | bytes 12988416 | tf_op jit(solution)/shard_map/sub | solution.py:63
  146.9 3.0 %fusion.3 = (f32[6,32,32,127]{3,2,1,0:T(8,128)S(1)}, f32[6,32,32,127]{3,2,1,0:T(8,128)}) fusion(f32[4,32,32,128]{3,2,1,0:T(8,128)S(1)} %get-tuple-element.13, f32[2,32,32,128]{3,2,1,0:T(8,128)S(1)} %fusion.49), kind=kLoop, calls=%fused_computation.29 | loop fusion | flops 1560576 | bytes 9388032 | tf_op jit(solution)/shard_map/concatenate | solution.py:74
  150.5 3.7 %fusion.2 = (f32[6,32,32,1]{3,2,1,0:T(8,128)}, f32[6,32,32,1]{3,2,1,0:T(8,128)}) fusion(f32[4,32,32,128]{3,2,1,0:T(8,128)S(1)} %get-tuple-element.13, f32[2,32,32,128]{3,2,1,0:T(8,128)S(1)} %fusion.49), kind=kLoop, calls=%fused_computation.28 | loop fusion | flops 12288 | bytes 3194880 | tf_op jit(solution)/shard_map/concatenate | solution.py:74
  154.2 3.4 %collective-permute-done.13 = f32[6,1,32,128]{3,2,1,0:T(8,128)S(1)} collective-permute-done((f32[6,1,32,128]{3,2,1,0:T(8,128)S(1)}, f32[6,1,32,128]{3,2,1,0:T(8,128)S(1)}, u32[]{:S(2)}, u32[]{:S(2)}) %collective-permute-start.13) | collective-permute-done | bytes 98336 | tf_op jit(solution)/shard_map/ppermute | solution.py:28
  164.5 7.3 %fusion.9 = f32[6,32,32,128]{3,2,1,0:T(8,128)S(1)} fusion(f32[2,32,32,128]{3,2,1,0:T(8,128)S(1)} %fusion.49, f32[4,32,32,128]{3,2,1,0:T(8,128)S(1)} %get-tuple-element.13, f32[6,34,1,128]{3,2,1,0:T(1,128)S(1)} %copy.23, f32[6,1,32,128]{3,2,1,0:T(8,128)S(1)} %collective-permute-done.12, f32[6,1,32,128]{3,2,1,0:T(8,128)S(1)} %collective-permute-done.13, ...), kind=kLoop, calls=%fused_computation.35 | loop fusion | flops 17301504 | bytes 12988416 | tf_op jit(solution)/shard_map/sub | solution.py:63
  (67 shorter events, 33.1 us)
Async XLA Ops:
  6.9 11.5 %copy-start = (f32[4,2]{0,1:T(2,128)S(1)}, f32[4,2]{0,1:T(2,128)}, u32[]{:S(2)}) copy-start(f32[4,2]{0,1:T(2,128)} %param.10) | copy-start | bytes 100
  6.9 11.5 %copy-start.1 = (f32[4]{0:T(128)S(1)}, f32[4]{0:T(128)}, u32[]{:S(2)}) copy-start(f32[4]{0:T(128)} %param.11) | copy-start | bytes 52
  10.6 24.0 %collective-permute-start = (f32[1,6,32,1024]{3,2,1,0:T(8,128)}, f32[1,6,32,1024]{3,2,1,0:T(8,128)}, u32[]{:S(2)}, u32[]{:S(2)}) collective-permute-start(f32[1,6,32,1024]{3,2,1,0:T(8,128)} %reshape.64), channel_id=1, source_target_pairs={{120,0},{124,4},{0,8},{4,12},{8,16},{12,20},{16,24},{20,28},{24,32... | collective-permute-start | bytes 2359304 | tf_op jit(solution)/shard_map/ppermute | solution.py:19
  12.2 29.9 %collective-permute-start.1 = (f32[1,6,32,1024]{3,2,1,0:T(8,128)}, f32[1,6,32,1024]{3,2,1,0:T(8,128)}, u32[]{:S(2)}, u32[]{:S(2)}) collective-permute-start(f32[1,6,32,1024]{3,2,1,0:T(8,128)} %reshape.64), channel_id=1, source_target_pairs={{124,0},{0,4},{4,8},{8,12},{12,16},{16,20},{20,24},{24,28},{28,32}... | collective-permute-start | bytes 2359304 | tf_op jit(solution)/shard_map/ppermute | solution.py:19
  12.2 33.2 %collective-permute-start.2 = (f32[1,6,32,1024]{3,2,1,0:T(8,128)}, f32[1,6,32,1024]{3,2,1,0:T(8,128)}, u32[]{:S(2)}, u32[]{:S(2)}) collective-permute-start(f32[1,6,32,1024]{3,2,1,0:T(8,128)} %reshape.64), channel_id=1, source_target_pairs={{4,0},{8,4},{12,8},{16,12},{20,16},{24,20},{28,24},{32,28},{36,32}... | collective-permute-start | bytes 2359304 | tf_op jit(solution)/shard_map/ppermute | solution.py:19
  17.3 31.4 %collective-permute-start.3 = (f32[1,6,32,1024]{3,2,1,0:T(8,128)}, f32[1,6,32,1024]{3,2,1,0:T(8,128)}, u32[]{:S(2)}, u32[]{:S(2)}) collective-permute-start(f32[1,6,32,1024]{3,2,1,0:T(8,128)} %reshape.64), channel_id=1, source_target_pairs={{8,0},{12,4},{16,8},{20,12},{24,16},{28,20},{32,24},{36,28},{40,32... | collective-permute-start | bytes 2359304 | tf_op jit(solution)/shard_map/ppermute | solution.py:19
  73.5 2.3 %collective-permute-start.4 = (f32[6,1,32,128]{3,2,1,0:T(8,128)S(1)}, f32[6,1,32,128]{3,2,1,0:T(8,128)S(1)}, u32[]{:S(2)}, u32[]{:S(2)}) collective-permute-start(f32[6,1,32,128]{3,2,1,0:T(8,128)S(1)} %get-tuple-element.42), channel_id=1, source_target_pairs={{4,0},{8,4},{12,8},{16,12},{20,16},{24,20},{28,24},{32,28},{36,32}... | collective-permute-start | bytes 294920 | tf_op jit(solution)/shard_map/ppermute | solution.py:31
  73.6 7.4 %collective-permute-start.5 = (f32[6,1,32,128]{3,2,1,0:T(8,128)S(1)}, f32[6,1,32,128]{3,2,1,0:T(8,128)S(1)}, u32[]{:S(2)}, u32[]{:S(2)}) collective-permute-start(f32[6,1,32,128]{3,2,1,0:T(8,128)S(1)} %get-tuple-element.41), channel_id=1, source_target_pairs={{0,4},{4,8},{8,12},{12,16},{16,20},{20,24},{24,28},{28,32},{32,36}... | collective-permute-start | bytes 294920 | tf_op jit(solution)/shard_map/ppermute | solution.py:28
  81.2 27.1 %collective-permute-start.6 = (f32[6,34,1,128]{3,1,2,0:T(8,128)S(1)}, f32[6,34,1,128]{3,1,2,0:T(8,128)S(1)}, u32[]{:S(2)}, u32[]{:S(2)}) collective-permute-start(f32[6,34,1,128]{3,1,2,0:T(8,128)S(1)} %copy.12), channel_id=1, source_target_pairs={{1,0},{2,1},{3,2},{0,3},{5,4},{6,5},{7,6},{4,7},{9,8},{10,9},{11,1... | collective-permute-start | bytes 313352 | tf_op jit(solution)/shard_map/ppermute | solution.py:31
  105.9 6.4 %collective-permute-start.7 = (f32[6,34,1,128]{3,1,2,0:T(8,128)S(1)}, f32[6,34,1,128]{3,1,2,0:T(8,128)S(1)}, u32[]{:S(2)}, u32[]{:S(2)}) collective-permute-start(f32[6,34,1,128]{3,1,2,0:T(8,128)S(1)} %copy.14), channel_id=1, source_target_pairs={{0,1},{1,2},{2,3},{3,0},{4,5},{5,6},{6,7},{7,4},{8,9},{9,10},{10,1... | collective-permute-start | bytes 313352 | tf_op jit(solution)/shard_map/ppermute | solution.py:28
  122.3 4.3 %collective-permute-start.8 = (f32[6,1,32,128]{3,2,1,0:T(8,128)S(1)}, f32[6,1,32,128]{3,2,1,0:T(8,128)S(1)}, u32[]{:S(2)}, u32[]{:S(2)}) collective-permute-start(f32[6,1,32,128]{3,2,1,0:T(8,128)S(1)} %get-tuple-element.36), channel_id=1, source_target_pairs={{4,0},{8,4},{12,8},{16,12},{20,16},{24,20},{28,24},{32,28},{36,32}... | collective-permute-start | bytes 294920 | tf_op jit(solution)/shard_map/ppermute | solution.py:31
  122.4 7.4 %collective-permute-start.9 = (f32[6,1,32,128]{3,2,1,0:T(8,128)S(1)}, f32[6,1,32,128]{3,2,1,0:T(8,128)S(1)}, u32[]{:S(2)}, u32[]{:S(2)}) collective-permute-start(f32[6,1,32,128]{3,2,1,0:T(8,128)S(1)} %get-tuple-element.35), channel_id=1, source_target_pairs={{0,4},{4,8},{8,12},{12,16},{16,20},{20,24},{24,28},{28,32},{32,36}... | collective-permute-start | bytes 294920 | tf_op jit(solution)/shard_map/ppermute | solution.py:28
  130.0 4.9 %collective-permute-start.10 = (f32[6,34,1,128]{3,1,2,0:T(8,128)S(1)}, f32[6,34,1,128]{3,1,2,0:T(8,128)S(1)}, u32[]{:S(2)}, u32[]{:S(2)}) collective-permute-start(f32[6,34,1,128]{3,1,2,0:T(8,128)S(1)} %copy.16), channel_id=1, source_target_pairs={{1,0},{2,1},{3,2},{0,3},{5,4},{6,5},{7,6},{4,7},{9,8},{10,9},{11,1... | collective-permute-start | bytes 313352 | tf_op jit(solution)/shard_map/ppermute | solution.py:31
  130.1 6.4 %collective-permute-start.11 = (f32[6,34,1,128]{3,1,2,0:T(8,128)S(1)}, f32[6,34,1,128]{3,1,2,0:T(8,128)S(1)}, u32[]{:S(2)}, u32[]{:S(2)}) collective-permute-start(f32[6,34,1,128]{3,1,2,0:T(8,128)S(1)} %copy.18), channel_id=1, source_target_pairs={{0,1},{1,2},{2,3},{3,0},{4,5},{5,6},{6,7},{7,4},{8,9},{9,10},{10,1... | collective-permute-start | bytes 313352 | tf_op jit(solution)/shard_map/ppermute | solution.py:28
  149.9 4.3 %collective-permute-start.12 = (f32[6,1,32,128]{3,2,1,0:T(8,128)S(1)}, f32[6,1,32,128]{3,2,1,0:T(8,128)S(1)}, u32[]{:S(2)}, u32[]{:S(2)}) collective-permute-start(f32[6,1,32,128]{3,2,1,0:T(8,128)S(1)} %get-tuple-element.30), channel_id=1, source_target_pairs={{4,0},{8,4},{12,8},{16,12},{20,16},{24,20},{28,24},{32,28},{36,32}... | collective-permute-start | bytes 294920 | tf_op jit(solution)/shard_map/ppermute | solution.py:31
  150.2 7.4 %collective-permute-start.13 = (f32[6,1,32,128]{3,2,1,0:T(8,128)S(1)}, f32[6,1,32,128]{3,2,1,0:T(8,128)S(1)}, u32[]{:S(2)}, u32[]{:S(2)}) collective-permute-start(f32[6,1,32,128]{3,2,1,0:T(8,128)S(1)} %get-tuple-element.29), channel_id=1, source_target_pairs={{0,4},{4,8},{8,12},{12,16},{16,20},{20,24},{24,28},{28,32},{32,36}... | collective-permute-start | bytes 294920 | tf_op jit(solution)/shard_map/ppermute | solution.py:28
  157.8 4.9 %collective-permute-start.14 = (f32[6,34,1,128]{3,1,2,0:T(8,128)S(1)}, f32[6,34,1,128]{3,1,2,0:T(8,128)S(1)}, u32[]{:S(2)}, u32[]{:S(2)}) collective-permute-start(f32[6,34,1,128]{3,1,2,0:T(8,128)S(1)} %copy.20), channel_id=1, source_target_pairs={{1,0},{2,1},{3,2},{0,3},{5,4},{6,5},{7,6},{4,7},{9,8},{10,9},{11,1... | collective-permute-start | bytes 313352 | tf_op jit(solution)/shard_map/ppermute | solution.py:31
  157.9 6.5 %collective-permute-start.15 = (f32[6,34,1,128]{3,1,2,0:T(8,128)S(1)}, f32[6,34,1,128]{3,1,2,0:T(8,128)S(1)}, u32[]{:S(2)}, u32[]{:S(2)}) collective-permute-start(f32[6,34,1,128]{3,1,2,0:T(8,128)S(1)} %copy.22), channel_id=1, source_target_pairs={{0,1},{1,2},{2,3},{3,0},{4,5},{5,6},{6,7},{7,4},{8,9},{9,10},{10,1... | collective-permute-start | bytes 313352 | tf_op jit(solution)/shard_map/ppermute | solution.py:28
where the time goes:
time: 177 us; the launch traced here: 176 us
  other arithmetic  48.4 us (27%)
  waiting for transfers between devices  46.6 us (26%)
  local copies, waits for them, and re-layouts  40.5 us (23%)
  starting transfers between devices  38.6 us (22%)
  between operations  2.27 us (1%)
    ppermute x6, starting transfers between devices, extended_2(): lax.ppermute(lax.slice_in_dim(block, 0, width, axis=dim), axis, backward)  25.3 us
    ppermute x4, waiting for transfers between devices, passed_along(): return lax.ppermute(block, axis, route)  20.5 us
    sub x3, other arithmetic, advance(): extended[:, 2:, 1:-1] + extended[:, :-2, 1:-1] + extended[:, 1:-1, 2:]  18.9 us
    ppermute x6, waiting for transfers between devices, extended_2(): lax.ppermute(lax.slice_in_dim(block, block.shape[dim] - width, None, axis...  18.7 us
    dynamic_update_slice x1, local copies, waits for them, and re-layouts, shards(): lax.dynamic_update_slice_in_dim(fields, arrived.reshape(6, edge, edge, ed...  15 us
    concatenate x6, other arithmetic, advance(): return jnp.concatenate([new_phase, new_potent], 0)  14.2 us
    squeeze x4, local copies, waits for them, and re-layouts, shards(): arrived = jnp.where(offset == distance, received[0], arrived)  13 us
    ppermute x6, waiting for transfers between devices, extended_2(): lax.ppermute(lax.slice_in_dim(block, 0, width, axis=dim), axis, backward)  7.48 us
  transfers between devices with their start and end apart: 16, of which 12 were waited for; matrix products, arithmetic and copies ran while one was open for 11% of the time, Pallas kernels for 0%

commit v1 on v0

v1 whole, which is shorter than its diff:
```python
import functools

import jax
import jax.numpy as jnp
from jax import lax
from jax.experimental import pallas as pl
from jax.experimental.pallas import tpu as pltpu
from jax.sharding import PartitionSpec as P

MESH = pl.DeviceIdType.MESH
ROW0 = 12
ROWS = 56
PLANES = 38


def constants(latent):
    lane = lax.broadcasted_iota(jnp.int32, (8, 128), 1)
    theta = 4.0 * (lane.astype(jnp.float32) + 0.5) / 128.0 - 2.0
    base = [1.8 + (1.2 * latent[a]) * theta for a in range(4)]
    return lane == 0, lane == 127, base


def tile_step(get, conc, base, first, last):
    cen = [get(c, 0, 0) for c in range(6)]
    near = []
    for c in range(6):
        f = cen[c]
        zp = jnp.where(last, f, pltpu.roll(f, 127, 1))
        zm = jnp.where(first, f, pltpu.roll(f, 1, 1))
        near.append(
            ((get(c, 1, 0) + get(c, -1, 0)) + (get(c, 0, 1) + get(c, 0, -1))) + (zp + zm)
        )
    rate = []
    for a in range(4):
        p = cen[a]
        q = p - p * p
        e = (1.2 * conc[a, 0]) * cen[4] + (1.2 * conc[a, 1]) * cen[5] + (base[a] - 3.6 * p)
        rate.append((0.1 * near[a] - 0.6 * p) - q * e)
    mean = 0.25 * ((rate[0] + rate[1]) + (rate[2] + rate[3]))
    change = [r - mean for r in rate]
    out = [cen[a] + change[a] for a in range(4)]
    for k in range(2):
        source = (conc[0, k] * change[0] + conc[1, k] * change[1]) + (
            conc[2, k] * change[2] + conc[3, k] * change[3]
        )
        out.append((0.4 * cen[4 + k] + 0.1 * near[4 + k]) - source)
    return out


def kernel(
    leaving, arriving, conc, latent, phases, potentials, out_phases, out_potentials,
    A, B, C, OUT, PK, SIB, SR, SL, RR, RL, META, META_R, META_L,
    in_sem, out_sem, meta_send, meta_recv, sib_send, sib_recv,
    r_send, r_recv, l_send, l_recv, up_send, up_recv, dn_send, dn_recv, x_send, x_recv,
):
    w, n = lax.axis_index("wide"), lax.axis_index("narrow")
    columns, rows = lax.axis_size("wide"), lax.axis_size("narrow")
    core = w % 2
    chip = w // 2
    sib = w + 1 - 2 * core
    right, left = (w + 2) % columns, (w + columns - 2) % columns
    after, before = (w + 1) % columns, (w + columns - 1) % columns
    up, down = (n + 1) % rows, (n + rows - 1) % rows

    def piece_of(i):
        return (i + 7) % 8

    def inputs(p):
        x = pl.ds(4 * p, 4)
        to = pl.ds(4 * p + 3, 4)
        rr = pl.ds(ROW0, 32)
        return (
            pltpu.make_async_copy(phases.at[:, x], A.at[0:4, to, rr], in_sem.at[0, p]),
            pltpu.make_async_copy(potentials.at[:, x], A.at[4:6, to, rr], in_sem.at[1, p]),
        )

    @pl.loop(0, 8)
    def _(i):
        for copy in inputs(piece_of(i)):
            copy.start()

    barrier = pltpu.get_barrier_semaphore()
    for device in ((right, n), (left, n), (after, n), (before, n), (w, up), (w, down)):
        pl.semaphore_signal(barrier, inc=1, device_id=device, device_id_type=MESH)

    slot = leaving[0, 0]
    source = arriving[0, 0]
    META[...] = jnp.full((8, 128), source, jnp.int32)
    lane = lax.broadcasted_iota(jnp.int32, (8, 128), 1)
    group = lane // 32

    pl.semaphore_wait(barrier, 6)

    def remote(src, dst, send, recv, device):
        return pltpu.make_async_remote_copy(
            src_ref=src, dst_ref=dst, send_sem=send, recv_sem=recv,
            device_id=device, device_id_type=MESH,
        )

    metas = (
        remote(META, META_R, meta_send.at[0], meta_recv.at[0], (left, n)),
        remote(META, META_L, meta_send.at[1], meta_recv.at[1], (right, n)),
    )
    for copy in metas:
        copy.start()

    def to_sib(p):
        return remote(PK.at[p], SIB.at[p], sib_send.at[p], sib_recv.at[p], (sib, n))

    def to_right(p):
        return remote(SR.at[p], RL.at[p], r_send.at[p], r_recv.at[p], (right, n))

    def to_left(p):
        return remote(SL.at[p], RR.at[p], l_send.at[p], l_recv.at[p], (left, n))

    def to_up(h, x, count):
        xs = pl.ds(x, count)
        return remote(
            A.at[:, xs, pl.ds(ROW0 + 29, 3)], A.at[:, xs, pl.ds(ROW0 - 3, 3)],
            up_send.at[h], up_recv.at[h], (w, up),
        )

    def to_down(h, x, count):
        xs = pl.ds(x, count)
        return remote(
            A.at[:, xs, pl.ds(ROW0, 3)], A.at[:, xs, pl.ds(ROW0 + 32, 3)],
            dn_send.at[h], dn_recv.at[h], (w, down),
        )

    core_rows = pl.ds(ROW0, 32)
    to_after = remote(
        A.at[:, pl.ds(32, 3), core_rows], A.at[:, pl.ds(0, 3), core_rows],
        x_send.at[0], x_recv.at[0], (after, n),
    )
    to_before = remote(
        A.at[:, pl.ds(3, 3), core_rows], A.at[:, pl.ds(35, 3), core_rows],
        x_send.at[1], x_recv.at[1], (before, n),
    )

    def pack(i):
        p = piece_of(i)
        for copy in inputs(p):
            copy.wait()
        shifts = [(32 * g + 128 - 32 * slot) % 128 for g in range(4)]

        @pl.loop(0, 6)
        def _(c):
            for t in range(4):
                r = pl.ds(ROW0 + 8 * t, 8)
                v = [pltpu.roll(A[c, 4 * p + 3 + g, r, :], shifts[g], 1) for g in range(4)]
                low = jnp.where(group == 0, v[0], v[1])
                high = jnp.where(group == 2, v[2], v[3])
                PK[p, c, pl.ds(8 * t, 8), :] = jnp.where(group < 2, low, high)

        to_sib(p).start()

    def route(i):
        p = piece_of(i)
        to_sib(p).wait_recv()
        go_right = META_R[...] == sib
        go_left = META_L[...] == sib

        @pl.loop(0, 6)
        def _(c):
            for t in range(4):
                r = pl.ds(8 * t, 8)
                own, other = PK[p, c, r, :], SIB[p, c, r, :]
                SR[p, c, r, :] = jnp.where(go_right, other, own)
                SL[p, c, r, :] = jnp.where(go_left, other, own)

        to_right(p).start()
        to_left(p).start()

    from_col = jnp.full((8, 128), source, jnp.int32)
    from_own = from_col == w
    from_sib = from_col == sib
    left_col = (w - core + columns - 2) % columns
    from_left = (from_col == left_col) | (from_col == left_col + 1)
    target = group == jnp.full((8, 128), slot, jnp.int32)

    def merge(i):
        p = piece_of(i)
        to_right(p).wait_recv()
        to_left(p).wait_recv()
        shifts = [(128 + 32 * slot - 32 * g) % 128 for g in range(4)]

        @pl.loop(0, 6)
        def _(c):
            for t in range(4):
                r = pl.ds(8 * t, 8)
                v = jnp.where(from_left, RL[p, c, r, :], RR[p, c, r, :])
                v = jnp.where(from_sib, SIB[p, c, r, :], v)
                v = jnp.where(from_own, PK[p, c, r, :], v)
                for g in range(4):
                    x, rr = 4 * p + 3 + g, pl.ds(ROW0 + 8 * t, 8)
                    A[c, x, rr, :] = jnp.where(target, pltpu.roll(v, shifts[g], 1), A[c, x, rr, :])

        to_up(p, 4 * p + 3, 4).start()
        to_down(p, 4 * p + 3, 4).start()

    pl.loop(0, 2)(pack)
    for copy in metas:
        copy.wait_recv()

    @pl.loop(2, 8)
    def _(i):
        pack(i)
        route(i - 2)

    pl.loop(6, 8)(route)

    first, last, base = constants(latent)

    def sweep(src, dst, x0, x1, tiles, row0, plane_off, row_off):
        @pl.loop(x0, x1)
        def _(x):
            for t in range(tiles):
                i = row0 + 8 * t

                def get(c, dx, dy):
                    return src[c, x + dx, pl.ds(i + dy, 8), :]

                out = tile_step(get, conc, base, first, last)
                for c in range(6):
                    dst[c, x - plane_off, pl.ds(i - row_off, 8), :] = out[c]

    def outputs(h, x, count):
        xs = pl.ds(x, count)
        return (
            pltpu.make_async_copy(OUT.at[0:4, xs], out_phases.at[:, xs], out_sem.at[0, h]),
            pltpu.make_async_copy(OUT.at[4:6, xs], out_potentials.at[:, xs], out_sem.at[1, h]),
        )

    def steps(h, a0, a1, b0, b1, c0, c1, count):
        sweep(A, B, a0 + 3, a1 + 3, 5, 8, 0, 0)
        sweep(B, C, b0 + 3, b1 + 3, 5, 8, 0, 0)
        sweep(C, OUT, c0 + 3, c1 + 3, 4, ROW0, 3, ROW0)
        for copy in outputs(h, c0, count):
            copy.start()

    def halo_wait(h, x, count):
        to_up(h, x, count).wait_recv()
        to_down(h, x, count).wait_recv()

    merge(0)
    to_after.start()
    merge(1)
    to_before.start()
    merge(2)
    to_after.wait_recv()
    to_up(8, 0, 3).start()
    to_down(8, 0, 3).start()
    to_before.wait_recv()
    to_up(9, 35, 3).start()
    to_down(9, 35, 3).start()

    halo_wait(0, 3, 4)
    halo_wait(8, 0, 3)
    steps(0, -2, 3, -1, 2, 0, 1, 1)

    @pl.loop(3, 8)
    def _(i):
        merge(i)
        q = i - 2
        halo_wait(q, 4 * q + 3, 4)
        steps(q, 4 * q - 1, 4 * q + 3, 4 * q - 2, 4 * q + 2, 4 * q - 3, 4 * q + 1, 4)

    halo_wait(6, 27, 4)
    halo_wait(7, 31, 4)
    halo_wait(9, 35, 3)
    steps(6, 23, 34, 22, 33, 21, 32, 11)

    for copy in metas:
        copy.wait_send()
    to_after.wait_send()
    to_before.wait_send()

    @pl.loop(0, 8)
    def _(p):
        to_sib(p).wait_send()
        to_right(p).wait_send()
        to_left(p).wait_send()
        to_up(p, 4 * p + 3, 4).wait_send()
        to_down(p, 4 * p + 3, 4).wait_send()

    for h, x in ((8, 0), (9, 35)):
        to_up(h, x, 3).wait_send()
        to_down(h, x, 3).wait_send()
    for copy in outputs(0, 0, 1) + outputs(6, 21, 11):
        copy.wait()

    @pl.loop(1, 6)
    def _(q):
        for copy in outputs(q, 4 * q - 3, 4):
            copy.wait()


def shards(phases, potentials, leaving, arriving, conc, latent):
    f32, i32 = jnp.float32, jnp.int32
    smem = pl.BlockSpec(memory_space=pltpu.SMEM)
    hbm = pl.BlockSpec(memory_space=pl.ANY)
    ext = pltpu.VMEM((6, PLANES, ROWS, 128), f32)
    block = pltpu.VMEM((8, 6, 32, 128), f32)
    meta = pltpu.VMEM((8, 128), i32)
    dma = pltpu.SemaphoreType.DMA
    return tuple(
        pl.pallas_call(
            kernel,
            out_shape=(
                jax.ShapeDtypeStruct(phases.shape, f32),
                jax.ShapeDtypeStruct(potentials.shape, f32),
            ),
            in_specs=[smem] * 4 + [hbm] * 2,
            out_specs=(hbm, hbm),
            scratch_shapes=[
                ext, ext, ext, pltpu.VMEM((6, 32, 32, 128), f32),
                block, block, block, block, block, block, meta, meta, meta,
                dma((2, 8)), dma((2, 8)), dma((2,)), dma((2,)), dma((8,)), dma((8,)),
                dma((8,)), dma((8,)), dma((8,)), dma((8,)),
                dma((10,)), dma((10,)), dma((10,)), dma((10,)), dma((2,)), dma((2,)),
            ],
            compiler_params=pltpu.CompilerParams(
                collective_id=0, has_side_effects=True, vmem_limit_bytes=50 * 2**20
            ),
            cost_estimate=pl.CostEstimate(
                flops=60_000_000, bytes_accessed=6_400_000, transcendentals=0
            ),
        )(leaving, arriving, conc, latent, phases, potentials)
    )


def solution(mesh):
    field = P(None, "wide", "narrow", None)
    in_specs = (field, field, P("wide", "narrow"), P("wide", "narrow"), P(), P())
    return jax.shard_map(
        shards, mesh=mesh, in_specs=in_specs, out_specs=(field, field), check_vma=False
    )
```

time: 177 us -> 70.4 us (0.40)
  Pallas kernels: 0 us -> 61.5 us
  other arithmetic: 48.4 us -> 0 us
  waiting for transfers between devices: 46.6 us -> 0 us
  starting transfers between devices: 38.6 us -> 0 us
  local copies, waits for them, and re-layouts: 40.5 us -> 6.69 us
    pallas_call x0 -> x1, Pallas kernels: none -> 61.5 us  [shards(): pl.pallas_call(kernel, out_shape=(jax.ShapeDtypeStruct(phases.shape, f32)...]
    ppermute x16 -> x0, waiting for transfers between devices: 46.6 us -> none  [the longest x4 20.5 us: passed_along(): return lax.ppermute(block, axis, route)]
    ppermute x16 -> x0, starting transfers between devices: 38.6 us -> none  [the longest x6 25.3 us: extended_2(): lax.ppermute(lax.slice_in_dim(block, 0, width, axis=dim), axis, backward)]
    sub x7 -> x0, other arithmetic: 21 us -> none  [the longest x3 18.9 us: advance(): extended[:, 2:, 1:-1] + extended[:, :-2, 1:-1] + extended[:, 1:-1, 2:]]
    dynamic_update_slice x1 -> x0, local copies, waits for them, and re-layouts: 15 us -> none  [shards(): lax.dynamic_update_slice_in_dim(fields, arrived.reshape(6, edge, edge, ed...]
    concatenate x6 -> x0, other arithmetic: 14.2 us -> none  [advance(): return jnp.concatenate([new_phase, new_potent], 0)]
    squeeze x4 -> x0, local copies, waits for them, and re-layouts: 13 us -> none  [shards(): arrived = jnp.where(offset == distance, received[0], arrived)]
    reduce_sum x6 -> x0, other arithmetic: 7.12 us -> none  [the longest x3 3.64 us: update(): rate = rate - jnp.mean(rate, axis=0, keepdims=True)]
  transfers between devices with their start and end apart: 16 -> 0, of which waited for: 12 -> 0; matrix products, arithmetic and copies ran while one was open for 11% -> 0% of each run, Pallas kernels for 0% -> 0%
where the time goes in v1:
time: 70.4 us; the launch traced here: 70.2 us
  Pallas kernels  61.5 us (87%)
  local copies, waits for them, and re-layouts  6.69 us (10%)
  between operations  1.93 us (3%)
    pallas_call x1, Pallas kernels, shards(): pl.pallas_call(kernel, out_shape=(jax.ShapeDtypeStruct(phases.shape, f32)...  61.5 us
    unnamed x7, local copies, waits for them, and re-layouts  6.69 us

profile of v1, /device:TPU:0, one launch (start us, length us, event | category | flops | bytes accessed | tf_op | source)
XLA Modules:
  0.0 70.2 jit_solution(6033316264428059298)
XLA Ops:
  1.9 0.8 %copy.8.conc = f32[4,2]{1,0:T(4,128)S(1)} copy(f32[4,2]{0,1:T(2,128)} %param.10) | data formatting | bytes 64 | tf_op args[4]
  2.7 0.0 copy-start
  2.7 1.2 %copy-done = f32[2,32,32,128]{3,2,1,0:T(8,128)S(1)} copy-done((f32[2,32,32,128]{3,2,1,0:T(8,128)S(1)}, f32[2,32,32,128]{3,2,1,0:T(8,128)}, u32[]{:S(2)}) %copy-start) | copy-done | bytes 1048600
  3.9 0.0 copy-start.1
  3.9 0.7 copy-done.1
  4.6 61.5 %shard_map.77 = (f32[4,32,32,128]{3,2,1,0:T(8,128)}, f32[2,32,32,128]{3,2,1,0:T(8,128)S(1)}) custom-call(s32[1,1]{1,0:T(1,128)S(6)} %copy.11.leaving, s32[1,1]{1,0:T(1,128)S(6)} %copy.12.arriving, f32[4,2]{1,0:T(4,128)S(1)} %copy.8.conc, f32[4]{0:T(128)S(1)} %copy-done.1, f32[4,32,32,128]{3,2,1,0:T(8,128)} %phases.1, f32[2,32,32,128]{3,2,1,0:T(8,128)S(1)} %copy-done), custom_call_target="tpu_custom_call" | custom-call | flops 60000000 | bytes 6400000 | tf_op jit(solution)/shard_map/pallas_call | solution.py:307
  66.1 3.1 %copy.13 = f32[4,32,32,128]{3,2,1,0:T(8,128)} copy(f32[4,32,32,128]{3,2,1,0:T(8,128)} %get-tuple-element.4) | data formatting | bytes 4194304
  69.2 1.0 %copy.14 = f32[2,32,32,128]{3,2,1,0:T(8,128)} copy(f32[2,32,32,128]{3,2,1,0:T(8,128)S(1)} %get-tuple-element.5) | data formatting | bytes 2097152
Async XLA Ops:
  2.7 1.2 %copy-start = (f32[2,32,32,128]{3,2,1,0:T(8,128)S(1)}, f32[2,32,32,128]{3,2,1,0:T(8,128)}, u32[]{:S(2)}) copy-start(f32[2,32,32,128]{3,2,1,0:T(8,128)} %potentials.1) | copy-start | bytes 3145732
  3.9 0.7 copy-start.1

commit v2 on v1

--- a/solution.py
+++ b/solution.py
@@ -13,14 +13,20 @@
 PLANES = 38
 
 
-def constants(latent):
+def constants(conc, latent):
     lane = lax.broadcasted_iota(jnp.int32, (8, 128), 1)
     theta = 4.0 * (lane.astype(jnp.float32) + 0.5) / 128.0 - 2.0
-    base = [1.8 + (1.2 * latent[a]) * theta for a in range(4)]
-    return lane == 0, lane == 127, base
-
-
-def tile_step(get, conc, base, first, last):
+    table = conc[...]
+    weight = [
+        [jnp.broadcast_to(table[k : k + 1, a : a + 1], (8, 128)) for k in range(2)]
+        for a in range(4)
+    ]
+    pull = [[1.2 * weight[a][k] for k in range(2)] for a in range(4)]
+    base = [1.8 + (1.2 * latent[0, a]) * theta for a in range(4)]
+    return lane == 0, lane == 127, base, weight, pull
+
+
+def tile_step(get, first, last, base, weight, pull):
     cen = [get(c, 0, 0) for c in range(6)]
     near = []
     for c in range(6):
@@ -34,14 +40,14 @@
     for a in range(4):
         p = cen[a]
         q = p - p * p
-        e = (1.2 * conc[a, 0]) * cen[4] + (1.2 * conc[a, 1]) * cen[5] + (base[a] - 3.6 * p)
+        e = pull[a][0] * cen[4] + pull[a][1] * cen[5] + (base[a] - 3.6 * p)
         rate.append((0.1 * near[a] - 0.6 * p) - q * e)
     mean = 0.25 * ((rate[0] + rate[1]) + (rate[2] + rate[3]))
     change = [r - mean for r in rate]
     out = [cen[a] + change[a] for a in range(4)]
     for k in range(2):
-        source = (conc[0, k] * change[0] + conc[1, k] * change[1]) + (
-            conc[2, k] * change[2] + conc[3, k] * change[3]
+        source = (weight[0][k] * change[0] + weight[1][k] * change[1]) + (
+            weight[2][k] * change[2] + weight[3][k] * change[3]
         )
         out.append((0.4 * cen[4 + k] + 0.1 * near[4 + k]) - source)
     return out
@@ -49,8 +55,8 @@
 
 def kernel(
     leaving, arriving, conc, latent, phases, potentials, out_phases, out_potentials,
-    A, B, C, OUT, PK, SIB, SR, SL, RR, RL, META, META_R, META_L,
-    in_sem, out_sem, meta_send, meta_recv, sib_send, sib_recv,
+    A, B, C, CONC, PK, SIB, SR, SL, RR, RL, META, META_R, META_L,
+    in_sem, conc_sem, meta_send, meta_recv, sib_send, sib_recv,
     r_send, r_recv, l_send, l_recv, up_send, up_recv, dn_send, dn_recv, x_send, x_recv,
 ):
     w, n = lax.axis_index("wide"), lax.axis_index("narrow")
@@ -79,6 +85,8 @@
         for copy in inputs(piece_of(i)):
             copy.start()
 
+    conc_copy = pltpu.make_async_copy(conc, CONC, conc_sem)
+    conc_copy.start()
     barrier = pltpu.get_barrier_semaphore()
     for device in ((right, n), (left, n), (after, n), (before, n), (w, up), (w, down)):
         pl.semaphore_signal(barrier, inc=1, device_id=device, device_id_type=MESH)
@@ -202,16 +210,16 @@
     for copy in metas:
         copy.wait_recv()
 
-    @pl.loop(2, 8)
+    @pl.loop(2, 5)
     def _(i):
         pack(i)
         route(i - 2)
 
-    pl.loop(6, 8)(route)
-
-    first, last, base = constants(latent)
-
-    def sweep(src, dst, x0, x1, tiles, row0, plane_off, row_off):
+    pl.loop(5, 8)(pack)
+    conc_copy.wait()
+    consts = constants(CONC, latent)
+
+    def sweep(src, dst, x0, x1, tiles, row0):
         @pl.loop(x0, x1)
         def _(x):
             for t in range(tiles):
@@ -220,23 +228,27 @@
                 def get(c, dx, dy):
                     return src[c, x + dx, pl.ds(i + dy, 8), :]
 
-                out = tile_step(get, conc, base, first, last)
+                out = tile_step(get, *consts)
                 for c in range(6):
-                    dst[c, x - plane_off, pl.ds(i - row_off, 8), :] = out[c]
-
-    def outputs(h, x, count):
-        xs = pl.ds(x, count)
-        return (
-            pltpu.make_async_copy(OUT.at[0:4, xs], out_phases.at[:, xs], out_sem.at[0, h]),
-            pltpu.make_async_copy(OUT.at[4:6, xs], out_potentials.at[:, xs], out_sem.at[1, h]),
-        )
-
-    def steps(h, a0, a1, b0, b1, c0, c1, count):
-        sweep(A, B, a0 + 3, a1 + 3, 5, 8, 0, 0)
-        sweep(B, C, b0 + 3, b1 + 3, 5, 8, 0, 0)
-        sweep(C, OUT, c0 + 3, c1 + 3, 4, ROW0, 3, ROW0)
-        for copy in outputs(h, c0, count):
-            copy.start()
+                    dst[c, x, pl.ds(i, 8), :] = out[c]
+
+    def steps(a0, a1, b0, b1, c0, c1):
+        sweep(A, B, a0 + 3, a1 + 3, 5, 8)
+        sweep(B, C, b0 + 3, b1 + 3, 5, 8)
+
+        @pl.loop(c0, c1)
+        def _(x):
+            for t in range(4):
+                i = ROW0 + 8 * t
+
+                def get(c, dx, dy):
+                    return C[c, x + 3 + dx, pl.ds(i + dy, 8), :]
+
+                out = tile_step(get, *consts)
+                for c in range(4):
+                    out_phases[c, x, pl.ds(8 * t, 8), :] = out[c]
+                for c in range(2):
+                    out_potentials[c, x, pl.ds(8 * t, 8), :] = out[4 + c]
 
     def halo_wait(h, x, count):
         to_up(h, x, count).wait_recv()
@@ -244,31 +256,44 @@
 
     merge(0)
     to_after.start()
+    route(3)
     merge(1)
     to_before.start()
+    route(4)
     merge(2)
-    to_after.wait_recv()
-    to_up(8, 0, 3).start()
-    to_down(8, 0, 3).start()
-    to_before.wait_recv()
-    to_up(9, 35, 3).start()
-    to_down(9, 35, 3).start()
-
+    route(5)
     halo_wait(0, 3, 4)
+
+    @pl.loop(1, 6)
+    def _(q):
+        merge(q + 2)
+
+        @pl.when(q < 3)
+        def _():
+            route(q + 5)
+
+        @pl.when(q == 3)
+        def _():
+            to_after.wait_recv()
+            to_up(8, 0, 3).start()
+            to_down(8, 0, 3).start()
+            to_before.wait_recv()
+            to_up(9, 35, 3).start()
+            to_down(9, 35, 3).start()
+
+        halo_wait(q, 4 * q + 3, 4)
+        cut = 1 - (q + 6) // 8
+        steps(
+            4 * q - 1, 4 * q + 3, 4 * q - 2 + 2 * cut, 4 * q + 2, 4 * q - 3 + 4 * cut, 4 * q + 1
+        )
+
     halo_wait(8, 0, 3)
-    steps(0, -2, 3, -1, 2, 0, 1, 1)
-
-    @pl.loop(3, 8)
-    def _(i):
-        merge(i)
-        q = i - 2
-        halo_wait(q, 4 * q + 3, 4)
-        steps(q, 4 * q - 1, 4 * q + 3, 4 * q - 2, 4 * q + 2, 4 * q - 3, 4 * q + 1, 4)
-
-    halo_wait(6, 27, 4)
+    steps(-2, 3, -1, 4, 0, 5)
     halo_wait(7, 31, 4)
     halo_wait(9, 35, 3)
-    steps(6, 23, 34, 22, 33, 21, 32, 11)
+    steps(29, 34, 30, 33, 31, 32)
+    halo_wait(6, 27, 4)
+    steps(23, 29, 22, 30, 21, 31)
 
     for copy in metas:
         copy.wait_send()
@@ -286,46 +311,57 @@
     for h, x in ((8, 0), (9, 35)):
         to_up(h, x, 3).wait_send()
         to_down(h, x, 3).wait_send()
-    for copy in outputs(0, 0, 1) + outputs(6, 21, 11):
+
+
+def store(phases, potentials, out_phases, out_potentials, sem):
+    copies = [
+        pltpu.make_async_copy(phases, out_phases, sem.at[0]),
+        pltpu.make_async_copy(potentials, out_potentials, sem.at[1]),
+    ]
+    for copy in copies:
+        copy.start()
+    for copy in copies:
         copy.wait()
-
-    @pl.loop(1, 6)
-    def _(q):
-        for copy in outputs(q, 4 * q - 3, 4):
-            copy.wait()
 
 
 def shards(phases, potentials, leaving, arriving, conc, latent):
     f32, i32 = jnp.float32, jnp.int32
     smem = pl.BlockSpec(memory_space=pltpu.SMEM)
-    hbm = pl.BlockSpec(memory_space=pl.ANY)
+    hbm = pl.BlockSpec(memory_space=pltpu.HBM)
+    vmem = pl.BlockSpec(memory_space=pltpu.VMEM)
     ext = pltpu.VMEM((6, PLANES, ROWS, 128), f32)
     block = pltpu.VMEM((8, 6, 32, 128), f32)
     meta = pltpu.VMEM((8, 128), i32)
     dma = pltpu.SemaphoreType.DMA
+    shapes = (phases.shape, potentials.shape)
+    results = pl.pallas_call(
+        kernel,
+        out_shape=tuple(pltpu.VMEM(s, f32) for s in shapes),
+        in_specs=[smem, smem, hbm, smem, hbm, hbm],
+        out_specs=(vmem, vmem),
+        scratch_shapes=[
+            ext, ext, ext, pltpu.VMEM((2, 4), f32),
+            block, block, block, block, block, block, meta, meta, meta,
+            dma((2, 8)), dma, dma((2,)), dma((2,)), dma((8,)), dma((8,)),
+            dma((8,)), dma((8,)), dma((8,)), dma((8,)),
+            dma((10,)), dma((10,)), dma((10,)), dma((10,)), dma((2,)), dma((2,)),
+        ],
+        compiler_params=pltpu.CompilerParams(
+            collective_id=0, has_side_effects=True, vmem_limit_bytes=60 * 2**20
+        ),
+        cost_estimate=pl.CostEstimate(
+            flops=60_000_000, bytes_accessed=6_400_000, transcendentals=0
+        ),
+    )(leaving, arriving, conc.T, latent.reshape(1, 4), phases, potentials)
     return tuple(
         pl.pallas_call(
-            kernel,
-            out_shape=(
-                jax.ShapeDtypeStruct(phases.shape, f32),
-                jax.ShapeDtypeStruct(potentials.shape, f32),
-            ),
-            in_specs=[smem] * 4 + [hbm] * 2,
+            store,
+            out_shape=tuple(jax.ShapeDtypeStruct(s, f32) for s in shapes),
+            in_specs=[vmem, vmem],
+            compiler_params=pltpu.CompilerParams(vmem_limit_bytes=2**18),
             out_specs=(hbm, hbm),
-            scratch_shapes=[
-                ext, ext, ext, pltpu.VMEM((6, 32, 32, 128), f32),
-                block, block, block, block, block, block, meta, meta, meta,
-                dma((2, 8)), dma((2, 8)), dma((2,)), dma((2,)), dma((8,)), dma((8,)),
-                dma((8,)), dma((8,)), dma((8,)), dma((8,)),
-                dma((10,)), dma((10,)), dma((10,)), dma((10,)), dma((2,)), dma((2,)),
-            ],
-            compiler_params=pltpu.CompilerParams(
-                collective_id=0, has_side_effects=True, vmem_limit_bytes=50 * 2**20
-            ),
-            cost_estimate=pl.CostEstimate(
-                flops=60_000_000, bytes_accessed=6_400_000, transcendentals=0
-            ),
-        )(leaving, arriving, conc, latent, phases, potentials)
+            scratch_shapes=[dma((2,))],
+        )(*results)
     )
 
 

time: 70.4 us -> 53.3 us (0.76)
  the two profiles are of different devices: /device:TPU:0 before, /device:TPU:1 now
where the time goes in v2:
time: 53.3 us; the launch traced here: 53.2 us
  Pallas kernels  51.3 us (96%)
  between operations  1.93 us (4%)
    pallas_call x1, Pallas kernels, shards(): pl.pallas_call(kernel, out_shape=tuple((pltpu.VMEM(s, f32) for s in shape...  49.6 us
    pallas_call x1, Pallas kernels, shards(): pl.pallas_call(store, out_shape=tuple((jax.ShapeDtypeStruct(s, f32) for s...  1.68 us

profile of v2, /device:TPU:1, one launch (start us, length us, event | category | flops | bytes accessed | tf_op | source)
XLA Modules:
  0.0 53.2 jit_solution(381985813284091724)
XLA Ops:
  1.9 49.6 %shard_map.77 = (f32[4,32,32,128]{3,2,1,0:T(8,128)S(1)}, f32[2,32,32,128]{3,2,1,0:T(8,128)S(1)}) custom-call(s32[1,1]{1,0:T(1,128)S(6)} %copy.8.leaving, s32[1,1]{1,0:T(1,128)S(6)} %copy.9.arriving, f32[2,4]{1,0:T(2,128)} %bitcast.2, f32[1,4]{1,0:T(1,128)} %bitcast.3, f32[4,32,32,128]{3,2,1,0:T(8,128)} %phases.1, f32[2,32,32,128]{3,2,1,0:T(8,128)} %potentials.1), custom_call_target="tpu_custom_call" | custom-call | flops 60000000 | bytes 6400000 | tf_op jit(solution)/shard_map/pallas_call | solution.py:337
  51.5 1.7 %shard_map.78 = (f32[4,32,32,128]{3,2,1,0:T(8,128)}, f32[2,32,32,128]{3,2,1,0:T(8,128)}) custom-call(f32[4,32,32,128]{3,2,1,0:T(8,128)S(1)} %get-tuple-element.4.phases, f32[2,32,32,128]{3,2,1,0:T(8,128)S(1)} %get-tuple-element.5.potentials), custom_call_target="tpu_custom_call" | custom-call | tf_op jit(solution)/shard_map/pallas_call | solution.py:357

commit v3 on v2

--- a/solution.py
+++ b/solution.py
@@ -11,6 +11,17 @@
 ROW0 = 12
 ROWS = 56
 PLANES = 38
+
+
+MXU = 4
+
+
+def neighbour_matrix():
+    row = lax.broadcasted_iota(jnp.int32, (256, 128), 0) % 128
+    col = lax.broadcasted_iota(jnp.int32, (256, 128), 1)
+    edge = (row == col) & ((row == 0) | (row == 127))
+    near = (row - col == 1) | (col - row == 1) | edge
+    return near.astype(jnp.float32).astype(jnp.bfloat16)
 
 
 def constants(conc, latent):
@@ -26,16 +37,18 @@
     return lane == 0, lane == 127, base, weight, pull
 
 
-def tile_step(get, first, last, base, weight, pull):
+def tile_step(get, along, first, last, base, weight, pull):
     cen = [get(c, 0, 0) for c in range(6)]
     near = []
     for c in range(6):
         f = cen[c]
-        zp = jnp.where(last, f, pltpu.roll(f, 127, 1))
-        zm = jnp.where(first, f, pltpu.roll(f, 1, 1))
-        near.append(
-            ((get(c, 1, 0) + get(c, -1, 0)) + (get(c, 0, 1) + get(c, 0, -1))) + (zp + zm)
-        )
+        if c < MXU:
+            z = along(c)
+        else:
+            zp = jnp.where(last, f, pltpu.roll(f, 127, 1))
+            zm = jnp.where(first, f, pltpu.roll(f, 1, 1))
+            z = zp + zm
+        near.append(((get(c, 1, 0) + get(c, -1, 0)) + (get(c, 0, 1) + get(c, 0, -1))) + z)
     rate = []
     for a in range(4):
         p = cen[a]
@@ -55,7 +68,7 @@
 
 def kernel(
     leaving, arriving, conc, latent, phases, potentials, out_phases, out_potentials,
-    A, B, C, CONC, PK, SIB, SR, SL, RR, RL, META, META_R, META_L,
+    A, B, C, NEAR, CONC, PK, SIB, SR, SL, RR, RL, META, META_R, META_L,
     in_sem, conc_sem, meta_send, meta_recv, sib_send, sib_recv,
     r_send, r_recv, l_send, l_recv, up_send, up_recv, dn_send, dn_recv, x_send, x_recv,
 ):
@@ -91,6 +104,7 @@
     for device in ((right, n), (left, n), (after, n), (before, n), (w, up), (w, down)):
         pl.semaphore_signal(barrier, inc=1, device_id=device, device_id_type=MESH)
 
+    NEAR[...] = neighbour_matrix()
     slot = leaving[0, 0]
     source = arriving[0, 0]
     META[...] = jnp.full((8, 128), source, jnp.int32)
@@ -219,36 +233,56 @@
     conc_copy.wait()
     consts = constants(CONC, latent)
 
-    def sweep(src, dst, x0, x1, tiles, row0):
-        @pl.loop(x0, x1)
-        def _(x):
+    def update(src, store, x0, planes, tiles, row0):
+        rows = 8 * tiles
+        f = jnp.concatenate(
+            [src[c, x0 + k, pl.ds(row0, rows), :] for k in range(planes) for c in range(MXU)], 0
+        )
+        high = f.astype(jnp.bfloat16)
+        low = (f - high.astype(jnp.float32)).astype(jnp.bfloat16)
+        sums = jnp.dot(
+            jnp.concatenate([high, low], 1), NEAR[...], preferred_element_type=jnp.float32
+        )
+        for k in range(planes):
+            x = x0 + k
             for t in range(tiles):
                 i = row0 + 8 * t
 
                 def get(c, dx, dy):
                     return src[c, x + dx, pl.ds(i + dy, 8), :]
 
-                out = tile_step(get, *consts)
-                for c in range(6):
-                    dst[c, x, pl.ds(i, 8), :] = out[c]
-
-    def steps(a0, a1, b0, b1, c0, c1):
-        sweep(A, B, a0 + 3, a1 + 3, 5, 8)
-        sweep(B, C, b0 + 3, b1 + 3, 5, 8)
-
-        @pl.loop(c0, c1)
-        def _(x):
-            for t in range(4):
-                i = ROW0 + 8 * t
-
-                def get(c, dx, dy):
-                    return C[c, x + 3 + dx, pl.ds(i + dy, 8), :]
-
-                out = tile_step(get, *consts)
-                for c in range(4):
-                    out_phases[c, x, pl.ds(8 * t, 8), :] = out[c]
-                for c in range(2):
-                    out_potentials[c, x, pl.ds(8 * t, 8), :] = out[4 + c]
+                def along(c):
+                    at = (k * MXU + c) * rows + 8 * t
+                    return sums[at : at + 8]
+
+                store(x, i, tile_step(get, along, *consts))
+
+    def into(dst):
+        def store(x, i, out):
+            for c in range(6):
+                dst[c, x, pl.ds(i, 8), :] = out[c]
+
+        return store
+
+    def result(x, i, out):
+        for c in range(4):
+            out_phases[c, x - 3, pl.ds(i - ROW0, 8), :] = out[c]
+        for c in range(2):
+            out_potentials[c, x - 3, pl.ds(i - ROW0, 8), :] = out[4 + c]
+
+    def chunked(src, store, x0, planes, tiles, row0):
+        size = planes if planes <= 6 else planes // 2
+        if size == planes:
+            update(src, store, x0, size, tiles, row0)
+        else:
+            @pl.loop(0, planes // size)
+            def _(j):
+                update(src, store, x0 + size * j, size, tiles, row0)
+
+    def steps(a, na, b, nb, c, nc):
+        chunked(A, into(B), a + 3, na, 5, 8)
+        chunked(B, into(C), b + 3, nb, 5, 8)
+        chunked(C, result, c + 3, nc, 4, ROW0)
 
     def halo_wait(h, x, count):
         to_up(h, x, count).wait_recv()
@@ -264,13 +298,18 @@
     route(5)
     halo_wait(0, 3, 4)
 
-    @pl.loop(1, 6)
+    merge(3)
+    route(6)
+    halo_wait(1, 7, 4)
+    steps(1, 6, 2, 4, 3, 2)
+
+    @pl.loop(2, 6)
     def _(q):
         merge(q + 2)
 
-        @pl.when(q < 3)
+        @pl.when(q == 2)
         def _():
-            route(q + 5)
+            route(7)
 
         @pl.when(q == 3)
         def _():
@@ -282,18 +321,15 @@
             to_down(9, 35, 3).start()
 
         halo_wait(q, 4 * q + 3, 4)
-        cut = 1 - (q + 6) // 8
-        steps(
-            4 * q - 1, 4 * q + 3, 4 * q - 2 + 2 * cut, 4 * q + 2, 4 * q - 3 + 4 * cut, 4 * q + 1
-        )
+        steps(4 * q - 1, 4, 4 * q - 2, 4, 4 * q - 3, 4)
 
     halo_wait(8, 0, 3)
-    steps(-2, 3, -1, 4, 0, 5)
+    steps(-2, 3, -1, 3, 0, 3)
     halo_wait(7, 31, 4)
     halo_wait(9, 35, 3)
-    steps(29, 34, 30, 33, 31, 32)
+    steps(29, 5, 30, 3, 31, 1)
     halo_wait(6, 27, 4)
-    steps(23, 29, 22, 30, 21, 31)
+    steps(23, 6, 22, 8, 21, 10)
 
     for copy in metas:
         copy.wait_send()
@@ -340,7 +376,7 @@
         in_specs=[smem, smem, hbm, smem, hbm, hbm],
         out_specs=(vmem, vmem),
         scratch_shapes=[
-            ext, ext, ext, pltpu.VMEM((2, 4), f32),
+            ext, ext, ext, pltpu.VMEM((256, 128), jnp.bfloat16), pltpu.VMEM((2, 4), f32),
             block, block, block, block, block, block, meta, meta, meta,
             dma((2, 8)), dma, dma((2,)), dma((2,)), dma((8,)), dma((8,)),
             dma((8,)), dma((8,)), dma((8,)), dma((8,)),

time: 53.3 us -> 49.2 us (0.923)
  the two profiles are of different devices: /device:TPU:1 before, /device:TPU:0 now
where the time goes in v3:
time: 49.2 us; the launch traced here: 48.3 us
  Pallas kernels  46.4 us (94%)
  between operations  1.93 us (4%)
    pallas_call x1, Pallas kernels, shards(): pl.pallas_call(kernel, out_shape=tuple((pltpu.VMEM(s, f32) for s in shape...  44.7 us
    pallas_call x1, Pallas kernels, shards(): pl.pallas_call(store, out_shape=tuple((jax.ShapeDtypeStruct(s, f32) for s...  1.68 us

profile of v3, /device:TPU:0, one launch (start us, length us, event | category | flops | bytes accessed | tf_op | source)
XLA Modules:
  0.0 48.3 jit_solution(291928001869973449)
XLA Ops:
  1.9 44.7 %shard_map.77 = (f32[4,32,32,128]{3,2,1,0:T(8,128)S(1)}, f32[2,32,32,128]{3,2,1,0:T(8,128)S(1)}) custom-call(s32[1,1]{1,0:T(1,128)S(6)} %copy.8.leaving, s32[1,1]{1,0:T(1,128)S(6)} %copy.9.arriving, f32[2,4]{1,0:T(2,128)} %bitcast.2, f32[1,4]{1,0:T(1,128)} %bitcast.3, f32[4,32,32,128]{3,2,1,0:T(8,128)} %phases.1, f32[2,32,32,128]{3,2,1,0:T(8,128)} %potentials.1), custom_call_target="tpu_custom_call" | custom-call | flops 60000000 | bytes 6400000 | tf_op jit(solution)/shard_map/pallas_call | solution.py:373
  46.7 1.7 %shard_map.78 = (f32[4,32,32,128]{3,2,1,0:T(8,128)}, f32[2,32,32,128]{3,2,1,0:T(8,128)}) custom-call(f32[4,32,32,128]{3,2,1,0:T(8,128)S(1)} %get-tuple-element.4.phases, f32[2,32,32,128]{3,2,1,0:T(8,128)S(1)} %get-tuple-element.5.potentials), custom_call_target="tpu_custom_call" | custom-call | tf_op jit(solution)/shard_map/pallas_call | solution.py:393

commit v4 on v3

--- a/solution.py
+++ b/solution.py
@@ -14,6 +14,10 @@
 
 
 MXU = 4
+
+
+EARLY = ((7, 0), (7, 1), (0, 0), (0, 1), (1, 0), (2, 0), (3, 0), (1, 1))
+LATE = ((4, 0), (2, 1), (5, 0), (3, 1), (6, 0), (4, 1), (5, 1), (6, 1))
 
 
 def neighbour_matrix():
@@ -67,9 +71,9 @@
 
 
 def kernel(
-    leaving, arriving, conc, latent, phases, potentials, out_phases, out_potentials,
-    A, B, C, NEAR, CONC, PK, SIB, SR, SL, RR, RL, META, META_R, META_L,
-    in_sem, conc_sem, meta_send, meta_recv, sib_send, sib_recv,
+    leaving_in, arriving_in, conc, latent, phases, potentials, out_phases, out_potentials,
+    A, B, C, NEAR, CONC, leaving, arriving, PK, TO_SIB, SIB, SR, SL, RR, RL, META, META_SIB, META_R, META_L,
+    in_sem, small_sem, meta_send, meta_recv, sib_send, sib_recv,
     r_send, r_recv, l_send, l_recv, up_send, up_recv, dn_send, dn_recv, x_send, x_recv,
 ):
     w, n = lax.axis_index("wide"), lax.axis_index("narrow")
@@ -81,9 +85,6 @@
     after, before = (w + 1) % columns, (w + columns - 1) % columns
     up, down = (n + 1) % rows, (n + rows - 1) % rows
 
-    def piece_of(i):
-        return (i + 7) % 8
-
     def inputs(p):
         x = pl.ds(4 * p, 4)
         to = pl.ds(4 * p + 3, 4)
@@ -95,24 +96,30 @@
 
     @pl.loop(0, 8)
     def _(i):
-        for copy in inputs(piece_of(i)):
+        for copy in inputs((i + 7) % 8):
             copy.start()
 
-    conc_copy = pltpu.make_async_copy(conc, CONC, conc_sem)
-    conc_copy.start()
+    small = [
+        pltpu.make_async_copy(src, dst, small_sem.at[i])
+        for i, (src, dst) in enumerate(
+            ((leaving_in, leaving), (arriving_in, arriving), (conc, CONC))
+        )
+    ]
+    for copy in small:
+        copy.start()
     barrier = pltpu.get_barrier_semaphore()
     for device in ((right, n), (left, n), (after, n), (before, n), (w, up), (w, down)):
         pl.semaphore_signal(barrier, inc=1, device_id=device, device_id_type=MESH)
 
     NEAR[...] = neighbour_matrix()
+    for copy in small:
+        copy.wait()
     slot = leaving[0, 0]
     source = arriving[0, 0]
     META[...] = jnp.full((8, 128), source, jnp.int32)
     lane = lax.broadcasted_iota(jnp.int32, (8, 128), 1)
     group = lane // 32
 
-    pl.semaphore_wait(barrier, 6)
-
     def remote(src, dst, send, recv, device):
         return pltpu.make_async_remote_copy(
             src_ref=src, dst_ref=dst, send_sem=send, recv_sem=recv,
@@ -120,20 +127,22 @@
         )
 
     metas = (
-        remote(META, META_R, meta_send.at[0], meta_recv.at[0], (left, n)),
-        remote(META, META_L, meta_send.at[1], meta_recv.at[1], (right, n)),
+        remote(META, META_SIB, meta_send.at[0], meta_recv.at[0], (sib, n)),
+        remote(META, META_R, meta_send.at[1], meta_recv.at[1], (left, n)),
+        remote(META, META_L, meta_send.at[2], meta_recv.at[2], (right, n)),
     )
-    for copy in metas:
-        copy.start()
-
-    def to_sib(p):
-        return remote(PK.at[p], SIB.at[p], sib_send.at[p], sib_recv.at[p], (sib, n))
-
-    def to_right(p):
-        return remote(SR.at[p], RL.at[p], r_send.at[p], r_recv.at[p], (right, n))
-
-    def to_left(p):
-        return remote(SL.at[p], RR.at[p], l_send.at[p], l_recv.at[p], (left, n))
+
+    def to_sib(p, h):
+        src = TO_SIB if (p, h) in EARLY else PK
+        return remote(src.at[p, h], SIB.at[p, h], sib_send.at[p, h], sib_recv.at[p, h], (sib, n))
+
+    def to_right(p, h):
+        src = PK if (p, h) in EARLY else SR
+        return remote(src.at[p, h], RL.at[p, h], r_send.at[p, h], r_recv.at[p, h], (right, n))
+
+    def to_left(p, h):
+        src = PK if (p, h) in EARLY else SL
+        return remote(src.at[p, h], RR.at[p, h], l_send.at[p, h], l_recv.at[p, h], (left, n))
 
     def to_up(h, x, count):
         xs = pl.ds(x, count)
@@ -159,78 +168,105 @@
         x_send.at[1], x_recv.at[1], (before, n),
     )
 
-    def pack(i):
-        p = piece_of(i)
+    tiles_of = ((0, 3), (1, 2))
+
+    def pack(p):
         for copy in inputs(p):
             copy.wait()
         shifts = [(32 * g + 128 - 32 * slot) % 128 for g in range(4)]
 
-        @pl.loop(0, 6)
-        def _(c):
-            for t in range(4):
-                r = pl.ds(ROW0 + 8 * t, 8)
-                v = [pltpu.roll(A[c, 4 * p + 3 + g, r, :], shifts[g], 1) for g in range(4)]
-                low = jnp.where(group == 0, v[0], v[1])
-                high = jnp.where(group == 2, v[2], v[3])
-                PK[p, c, pl.ds(8 * t, 8), :] = jnp.where(group < 2, low, high)
-
-        to_sib(p).start()
-
-    def route(i):
-        p = piece_of(i)
-        to_sib(p).wait_recv()
-        go_right = META_R[...] == sib
-        go_left = META_L[...] == sib
-
-        @pl.loop(0, 6)
-        def _(c):
-            for t in range(4):
-                r = pl.ds(8 * t, 8)
-                own, other = PK[p, c, r, :], SIB[p, c, r, :]
-                SR[p, c, r, :] = jnp.where(go_right, other, own)
-                SL[p, c, r, :] = jnp.where(go_left, other, own)
-
-        to_right(p).start()
-        to_left(p).start()
+        for c in range(6):
+            for h in range(2):
+                for k, t in enumerate(tiles_of[h]):
+                    r = pl.ds(ROW0 + 8 * t, 8)
+                    v = [pltpu.roll(A[c, 4 * p + 3 + g, r, :], shifts[g], 1) for g in range(4)]
+                    low = jnp.where(group == 0, v[0], v[1])
+                    high = jnp.where(group == 2, v[2], v[3])
+                    PK[p, h, c, pl.ds(8 * k, 8), :] = jnp.where(group < 2, low, high)
+
+    def send(p, h):
+        to_right(p, h).start()
+        to_left(p, h).start()
 
     from_col = jnp.full((8, 128), source, jnp.int32)
-    from_own = from_col == w
+    from_own, from_left, from_right = from_col == w, from_col == left, from_col == right
     from_sib = from_col == sib
-    left_col = (w - core + columns - 2) % columns
-    from_left = (from_col == left_col) | (from_col == left_col + 1)
+    from_left_chip = from_left | (from_col == (sib + columns - 2) % columns)
     target = group == jnp.full((8, 128), slot, jnp.int32)
 
-    def merge(i):
-        p = piece_of(i)
-        to_right(p).wait_recv()
-        to_left(p).wait_recv()
+    def forward(p, h):
+        to_right(p, h).wait_recv()
+        to_left(p, h).wait_recv()
+        want = META_SIB[...]
+        own, from_l = want == w, want == left
+
+        for c in range(6):
+            for k in range(2):
+                r = pl.ds(8 * k, 8)
+                v = jnp.where(from_l, RL[p, h, c, r, :], RR[p, h, c, r, :])
+                TO_SIB[p, h, c, r, :] = jnp.where(own, PK[p, h, c, r, :], v)
+
+        to_sib(p, h).start()
+
+    def route(p, h):
+        to_sib(p, h).wait_recv()
+        go_right, go_left = META_R[...] == sib, META_L[...] == sib
+        for c in range(6):
+            for k in range(2):
+                r = pl.ds(8 * k, 8)
+                own, other = PK[p, h, c, r, :], SIB[p, h, c, r, :]
+                SR[p, h, c, r, :] = jnp.where(go_right, other, own)
+                SL[p, h, c, r, :] = jnp.where(go_left, other, own)
+        send(p, h)
+
+    def merge(p, h):
+        if (p, h) in EARLY:
+            to_sib(p, h).wait_recv()
+        else:
+            to_right(p, h).wait_recv()
+            to_left(p, h).wait_recv()
         shifts = [(128 + 32 * slot - 32 * g) % 128 for g in range(4)]
 
-        @pl.loop(0, 6)
-        def _(c):
-            for t in range(4):
-                r = pl.ds(8 * t, 8)
-                v = jnp.where(from_left, RL[p, c, r, :], RR[p, c, r, :])
-                v = jnp.where(from_sib, SIB[p, c, r, :], v)
-                v = jnp.where(from_own, PK[p, c, r, :], v)
+        for c in range(6):
+            for k, t in enumerate(tiles_of[h]):
+                r = pl.ds(8 * k, 8)
+                if (p, h) in EARLY:
+                    v = jnp.where(from_left, RL[p, h, c, r, :], SIB[p, h, c, r, :])
+                    v = jnp.where(from_right, RR[p, h, c, r, :], v)
+                else:
+                    v = jnp.where(from_left_chip, RL[p, h, c, r, :], RR[p, h, c, r, :])
+                    v = jnp.where(from_sib, SIB[p, h, c, r, :], v)
+                v = jnp.where(from_own, PK[p, h, c, r, :], v)
                 for g in range(4):
                     x, rr = 4 * p + 3 + g, pl.ds(ROW0 + 8 * t, 8)
                     A[c, x, rr, :] = jnp.where(target, pltpu.roll(v, shifts[g], 1), A[c, x, rr, :])
 
-        to_up(p, 4 * p + 3, 4).start()
-        to_down(p, 4 * p + 3, 4).start()
-
-    pl.loop(0, 2)(pack)
+        if h == 0:
+            to_up(p, 4 * p + 3, 4).start()
+            to_down(p, 4 * p + 3, 4).start()
+
+    pack(7)
+    pl.semaphore_wait(barrier, 6)
+    send(7, 0)
+    send(7, 1)
+    for copy in metas:
+        copy.start()
+    pack(0)
+    send(0, 0)
+    send(0, 1)
+    pack(1)
+    send(1, 0)
+    pack(2)
+    send(2, 0)
+    pack(3)
+    send(3, 0)
+    send(1, 1)
+    pl.loop(4, 7)(pack)
+    for p, h in LATE:
+        to_sib(p, h).start()
     for copy in metas:
         copy.wait_recv()
 
-    @pl.loop(2, 5)
-    def _(i):
-        pack(i)
-        route(i - 2)
-
-    pl.loop(5, 8)(pack)
-    conc_copy.wait()
     consts = constants(CONC, latent)
 
     def update(src, store, x0, planes, tiles, row0):
@@ -288,46 +324,66 @@
         to_up(h, x, count).wait_recv()
         to_down(h, x, count).wait_recv()
 
-    merge(0)
+    forward(7, 0)
+    forward(7, 1)
+    forward(0, 0)
+    merge(7, 0)
+    merge(7, 1)
     to_after.start()
-    route(3)
-    merge(1)
+    forward(0, 1)
+    merge(0, 0)
+    forward(1, 0)
+    merge(0, 1)
     to_before.start()
-    route(4)
-    merge(2)
-    route(5)
+    for p, h in LATE:
+        route(p, h)
+    merge(1, 0)
+    forward(2, 0)
+    forward(3, 0)
+    merge(2, 0)
+    forward(1, 1)
+    merge(3, 0)
+    merge(1, 1)
     halo_wait(0, 3, 4)
-
-    merge(3)
-    route(6)
     halo_wait(1, 7, 4)
     steps(1, 6, 2, 4, 3, 2)
-
-    @pl.loop(2, 6)
-    def _(q):
-        merge(q + 2)
-
-        @pl.when(q == 2)
-        def _():
-            route(7)
-
-        @pl.when(q == 3)
-        def _():
-            to_after.wait_recv()
-            to_up(8, 0, 3).start()
-            to_down(8, 0, 3).start()
-            to_before.wait_recv()
-            to_up(9, 35, 3).start()
-            to_down(9, 35, 3).start()
-
-        halo_wait(q, 4 * q + 3, 4)
-        steps(4 * q - 1, 4, 4 * q - 2, 4, 4 * q - 3, 4)
-
+    to_after.wait_recv()
+    to_up(8, 0, 3).start()
+    to_down(8, 0, 3).start()
+    to_before.wait_recv()
+    to_up(9, 35, 3).start()
+    to_down(9, 35, 3).start()
+    merge(4, 0)
+    merge(2, 1)
     halo_wait(8, 0, 3)
     steps(-2, 3, -1, 3, 0, 3)
     halo_wait(7, 31, 4)
     halo_wait(9, 35, 3)
     steps(29, 5, 30, 3, 31, 1)
+
+    @pl.loop(2, 6)
+    def _(q):
+        halo_wait(q, 4 * q + 3, 4)
+        steps(4 * q - 1, 4, 4 * q - 2, 4, 4 * q - 3, 4)
+
+        @pl.when(q == 2)
+        def _():
+            merge(5, 0)
+            merge(3, 1)
+
+        @pl.when(q == 3)
+        def _():
+            merge(6, 0)
+            merge(4, 1)
+
+        @pl.when(q == 4)
+        def _():
+            merge(5, 1)
+
+        @pl.when(q == 5)
+        def _():
+            merge(6, 1)
+
     halo_wait(6, 27, 4)
     steps(23, 6, 22, 8, 21, 10)
 
@@ -336,11 +392,13 @@
     to_after.wait_send()
     to_before.wait_send()
 
+    for p, h in EARLY + LATE:
+        to_sib(p, h).wait_send()
+        to_right(p, h).wait_send()
+        to_left(p, h).wait_send()
+
     @pl.loop(0, 8)
     def _(p):
-        to_sib(p).wait_send()
-        to_right(p).wait_send()
-        to_left(p).wait_send()
         to_up(p, 4 * p + 3, 4).wait_send()
         to_down(p, 4 * p + 3, 4).wait_send()
 
@@ -366,20 +424,21 @@
     hbm = pl.BlockSpec(memory_space=pltpu.HBM)
     vmem = pl.BlockSpec(memory_space=pltpu.VMEM)
     ext = pltpu.VMEM((6, PLANES, ROWS, 128), f32)
-    block = pltpu.VMEM((8, 6, 32, 128), f32)
+    block = pltpu.VMEM((8, 2, 6, 16, 128), f32)
     meta = pltpu.VMEM((8, 128), i32)
     dma = pltpu.SemaphoreType.DMA
     shapes = (phases.shape, potentials.shape)
     results = pl.pallas_call(
         kernel,
         out_shape=tuple(pltpu.VMEM(s, f32) for s in shapes),
-        in_specs=[smem, smem, hbm, smem, hbm, hbm],
+        in_specs=[hbm, hbm, hbm, smem, hbm, hbm],
         out_specs=(vmem, vmem),
         scratch_shapes=[
             ext, ext, ext, pltpu.VMEM((256, 128), jnp.bfloat16), pltpu.VMEM((2, 4), f32),
-            block, block, block, block, block, block, meta, meta, meta,
-            dma((2, 8)), dma, dma((2,)), dma((2,)), dma((8,)), dma((8,)),
-            dma((8,)), dma((8,)), dma((8,)), dma((8,)),
+            pltpu.SMEM((1, 1), i32), pltpu.SMEM((1, 1), i32),
+            block, block, block, block, block, block, block, meta, meta, meta, meta,
+            dma((2, 8)), dma((3,)), dma((3,)), dma((3,)), dma((8, 2)), dma((8, 2)),
+            dma((8, 2)), dma((8, 2)), dma((8, 2)), dma((8, 2)),
             dma((10,)), dma((10,)), dma((10,)), dma((10,)), dma((2,)), dma((2,)),
         ],
         compiler_params=pltpu.CompilerParams(

time: 49.2 us -> 43.7 us (0.89); the launches traced: 48.3 us -> 43.6 us
  Pallas kernels: 46.4 us -> 41.7 us
    pallas_call x1, Pallas kernels: 44.7 us -> 40 us  [shards(): pl.pallas_call(kernel, out_shape=tuple((pltpu.VMEM(s, f32) for s in shape...]
where the time goes in v4:
time: 43.7 us; the launch traced here: 43.6 us
  Pallas kernels  41.7 us (95%)
  between operations  1.93 us (4%)
    pallas_call x1, Pallas kernels, shards(): pl.pallas_call(kernel, out_shape=tuple((pltpu.VMEM(s, f32) for s in shape...  40 us
    pallas_call x1, Pallas kernels, shards(): pl.pallas_call(store, out_shape=tuple((jax.ShapeDtypeStruct(s, f32) for s...  1.68 us

profile of v4, /device:TPU:0, one launch (start us, length us, event | category | flops | bytes accessed | tf_op | source)
XLA Modules:
  0.0 43.6 jit_solution(263507418714092251)
XLA Ops:
  1.9 40.0 %shard_map.77 = (f32[4,32,32,128]{3,2,1,0:T(8,128)S(1)}, f32[2,32,32,128]{3,2,1,0:T(8,128)S(1)}) custom-call(s32[1,1]{1,0:T(1,128)S(6)} %copy.8.leaving_in, s32[1,1]{1,0:T(1,128)S(6)} %copy.9.arriving_in, f32[2,4]{1,0:T(2,128)} %bitcast.2, f32[1,4]{1,0:T(1,128)} %bitcast.3, f32[4,32,32,128]{3,2,1,0:T(8,128)} %phases.1, f32[2,32,32,128]{3,2,1,0:T(8,128)} %potentials.1), custom_call_target="tpu_custom_call" | custom-call | flops 60000000 | bytes 6400000 | tf_op jit(solution)/shard_map/pallas_call | solution.py:431
  41.9 1.7 %shard_map.78 = (f32[4,32,32,128]{3,2,1,0:T(8,128)}, f32[2,32,32,128]{3,2,1,0:T(8,128)}) custom-call(f32[4,32,32,128]{3,2,1,0:T(8,128)S(1)} %get-tuple-element.4.phases, f32[2,32,32,128]{3,2,1,0:T(8,128)S(1)} %get-tuple-element.5.potentials), custom_call_target="tpu_custom_call" | custom-call | tf_op jit(solution)/shard_map/pallas_call | solution.py:452

commit v5 on v4

--- a/solution.py
+++ b/solution.py
@@ -16,8 +16,8 @@
 MXU = 4
 
 
-EARLY = ((7, 0), (7, 1), (0, 0), (0, 1), (1, 0), (2, 0), (3, 0), (1, 1))
-LATE = ((4, 0), (2, 1), (5, 0), (3, 1), (6, 0), (4, 1), (5, 1), (6, 1))
+EARLY = ((7, 0), (7, 1), (0, 0), (0, 1), (1, 0), (1, 1), (2, 0), (3, 0))
+LATE = ((2, 1), (4, 0), (3, 1), (5, 0), (4, 1), (6, 0), (5, 1), (6, 1))
 
 
 def neighbour_matrix():
@@ -94,24 +94,23 @@
             pltpu.make_async_copy(potentials.at[:, x], A.at[4:6, to, rr], in_sem.at[1, p]),
         )
 
+    small = [
+        pltpu.make_async_copy(src, dst, small_sem.at[i])
+        for i, (src, dst) in enumerate(
+            ((leaving_in, leaving), (arriving_in, arriving), (conc, CONC))
+        )
+    ]
+    for copy in small:
+        copy.start()
     @pl.loop(0, 8)
     def _(i):
         for copy in inputs((i + 7) % 8):
             copy.start()
 
-    small = [
-        pltpu.make_async_copy(src, dst, small_sem.at[i])
-        for i, (src, dst) in enumerate(
-            ((leaving_in, leaving), (arriving_in, arriving), (conc, CONC))
-        )
-    ]
-    for copy in small:
-        copy.start()
     barrier = pltpu.get_barrier_semaphore()
     for device in ((right, n), (left, n), (after, n), (before, n), (w, up), (w, down)):
         pl.semaphore_signal(barrier, inc=1, device_id=device, device_id_type=MESH)
 
-    NEAR[...] = neighbour_matrix()
     for copy in small:
         copy.wait()
     slot = leaving[0, 0]
@@ -158,15 +157,12 @@
             dn_send.at[h], dn_recv.at[h], (w, down),
         )
 
-    core_rows = pl.ds(ROW0, 32)
-    to_after = remote(
-        A.at[:, pl.ds(32, 3), core_rows], A.at[:, pl.ds(0, 3), core_rows],
-        x_send.at[0], x_recv.at[0], (after, n),
-    )
-    to_before = remote(
-        A.at[:, pl.ds(3, 3), core_rows], A.at[:, pl.ds(35, 3), core_rows],
-        x_send.at[1], x_recv.at[1], (before, n),
-    )
+    def to_side(side):
+        r = pl.ds(ROW0 - 3, 38)
+        return remote(
+            A.at[:, pl.ds(32 - 29 * side, 3), r], A.at[:, pl.ds(35 * side, 3), r],
+            x_send.at[side], x_recv.at[side], (after + side * (before - after), n),
+        )
 
     tiles_of = ((0, 3), (1, 2))
 
@@ -251,19 +247,14 @@
     send(7, 1)
     for copy in metas:
         copy.start()
-    pack(0)
-    send(0, 0)
-    send(0, 1)
-    pack(1)
-    send(1, 0)
-    pack(2)
-    send(2, 0)
-    pack(3)
-    send(3, 0)
-    send(1, 1)
+    for p, h in EARLY[2:]:
+        if h == 0:
+            pack(p)
+        send(p, h)
     pl.loop(4, 7)(pack)
     for p, h in LATE:
         to_sib(p, h).start()
+    NEAR[...] = neighbour_matrix()
     for copy in metas:
         copy.wait_recv()
 
@@ -306,19 +297,10 @@
         for c in range(2):
             out_potentials[c, x - 3, pl.ds(i - ROW0, 8), :] = out[4 + c]
 
-    def chunked(src, store, x0, planes, tiles, row0):
-        size = planes if planes <= 6 else planes // 2
-        if size == planes:
-            update(src, store, x0, size, tiles, row0)
-        else:
-            @pl.loop(0, planes // size)
-            def _(j):
-                update(src, store, x0 + size * j, size, tiles, row0)
-
     def steps(a, na, b, nb, c, nc):
-        chunked(A, into(B), a + 3, na, 5, 8)
-        chunked(B, into(C), b + 3, nb, 5, 8)
-        chunked(C, result, c + 3, nc, 4, ROW0)
+        update(A, into(B), a + 3, na, 5, 8)
+        update(B, into(C), b + 3, nb, 5, 8)
+        update(C, result, c + 3, nc, 4, ROW0)
 
     def halo_wait(h, x, count):
         to_up(h, x, count).wait_recv()
@@ -326,71 +308,67 @@
 
     forward(7, 0)
     forward(7, 1)
+    for p, h in LATE:
+        route(p, h)
     forward(0, 0)
     merge(7, 0)
     merge(7, 1)
-    to_after.start()
     forward(0, 1)
     merge(0, 0)
     forward(1, 0)
     merge(0, 1)
-    to_before.start()
-    for p, h in LATE:
-        route(p, h)
     merge(1, 0)
+    forward(1, 1)
     forward(2, 0)
+    merge(1, 1)
+    merge(2, 0)
     forward(3, 0)
-    merge(2, 0)
-    forward(1, 1)
-    merge(3, 0)
-    merge(1, 1)
+    halo_wait(7, 31, 4)
+    to_side(0).start()
     halo_wait(0, 3, 4)
+    to_side(1).start()
     halo_wait(1, 7, 4)
     steps(1, 6, 2, 4, 3, 2)
-    to_after.wait_recv()
-    to_up(8, 0, 3).start()
-    to_down(8, 0, 3).start()
-    to_before.wait_recv()
-    to_up(9, 35, 3).start()
-    to_down(9, 35, 3).start()
-    merge(4, 0)
+    merge(3, 0)
     merge(2, 1)
-    halo_wait(8, 0, 3)
-    steps(-2, 3, -1, 3, 0, 3)
-    halo_wait(7, 31, 4)
-    halo_wait(9, 35, 3)
-    steps(29, 5, 30, 3, 31, 1)
-
-    @pl.loop(2, 6)
+
+    @pl.loop(2, 8)
     def _(q):
-        halo_wait(q, 4 * q + 3, 4)
+        @pl.when(q < 7)
+        def _():
+            halo_wait(q, 4 * q + 3, 4)
+
         steps(4 * q - 1, 4, 4 * q - 2, 4, 4 * q - 3, 4)
 
         @pl.when(q == 2)
         def _():
-            merge(5, 0)
+            merge(4, 0)
             merge(3, 1)
 
         @pl.when(q == 3)
         def _():
-            merge(6, 0)
+            merge(5, 0)
             merge(4, 1)
 
         @pl.when(q == 4)
         def _():
+            merge(6, 0)
             merge(5, 1)
 
         @pl.when(q == 5)
         def _():
             merge(6, 1)
 
-    halo_wait(6, 27, 4)
-    steps(23, 6, 22, 8, 21, 10)
+    @pl.loop(0, 2)
+    def _(t):
+        side = core * t + (1 - core) * (1 - t)
+        to_side(side).wait_recv()
+        steps(33 * side - 2, 3, 31 * side - 1, 3, 29 * side, 3)
 
     for copy in metas:
         copy.wait_send()
-    to_after.wait_send()
-    to_before.wait_send()
+    to_side(0).wait_send()
+    to_side(1).wait_send()
 
     for p, h in EARLY + LATE:
         to_sib(p, h).wait_send()
@@ -401,10 +379,6 @@
     def _(p):
         to_up(p, 4 * p + 3, 4).wait_send()
         to_down(p, 4 * p + 3, 4).wait_send()
-
-    for h, x in ((8, 0), (9, 35)):
-        to_up(h, x, 3).wait_send()
-        to_down(h, x, 3).wait_send()
 
 
 def store(phases, potentials, out_phases, out_potentials, sem):
@@ -439,7 +413,7 @@
             block, block, block, block, block, block, block, meta, meta, meta, meta,
             dma((2, 8)), dma((3,)), dma((3,)), dma((3,)), dma((8, 2)), dma((8, 2)),
             dma((8, 2)), dma((8, 2)), dma((8, 2)), dma((8, 2)),
-            dma((10,)), dma((10,)), dma((10,)), dma((10,)), dma((2,)), dma((2,)),
+            dma((8,)), dma((8,)), dma((8,)), dma((8,)), dma((2,)), dma((2,)),
         ],
         compiler_params=pltpu.CompilerParams(
             collective_id=0, has_side_effects=True, vmem_limit_bytes=60 * 2**20

time: 43.7 us -> 42 us (0.961)
  Pallas kernels: 41.7 us -> 39.9 us
    pallas_call x1, Pallas kernels: 40 us -> 38.2 us  [shards(): pl.pallas_call(kernel, out_shape=tuple((pltpu.VMEM(s, f32) for s in shape...]
where the time goes in v5:
time: 42 us; the launch traced here: 41.8 us
  Pallas kernels  39.9 us (95%)
  between operations  1.93 us (5%)
    pallas_call x1, Pallas kernels, shards(): pl.pallas_call(kernel, out_shape=tuple((pltpu.VMEM(s, f32) for s in shape...  38.2 us
    pallas_call x1, Pallas kernels, shards(): pl.pallas_call(store, out_shape=tuple((jax.ShapeDtypeStruct(s, f32) for s...  1.68 us

profile of v5, /device:TPU:0, one launch (start us, length us, event | category | flops | bytes accessed | tf_op | source)
XLA Modules:
  0.0 41.8 jit_solution(2279163591619027549)
XLA Ops:
  1.9 38.2 %shard_map.77 = (f32[4,32,32,128]{3,2,1,0:T(8,128)S(1)}, f32[2,32,32,128]{3,2,1,0:T(8,128)S(1)}) custom-call(s32[1,1]{1,0:T(1,128)S(6)} %copy.8.leaving_in, s32[1,1]{1,0:T(1,128)S(6)} %copy.9.arriving_in, f32[2,4]{1,0:T(2,128)} %bitcast.2, f32[1,4]{1,0:T(1,128)} %bitcast.3, f32[4,32,32,128]{3,2,1,0:T(8,128)} %phases.1, f32[2,32,32,128]{3,2,1,0:T(8,128)} %potentials.1), custom_call_target="tpu_custom_call" | custom-call | flops 60000000 | bytes 6400000 | tf_op jit(solution)/shard_map/pallas_call | solution.py:405
  40.1 1.7 %shard_map.78 = (f32[4,32,32,128]{3,2,1,0:T(8,128)}, f32[2,32,32,128]{3,2,1,0:T(8,128)}) custom-call(f32[4,32,32,128]{3,2,1,0:T(8,128)S(1)} %get-tuple-element.4.phases, f32[2,32,32,128]{3,2,1,0:T(8,128)S(1)} %get-tuple-element.5.potentials), custom_call_target="tpu_custom_call" | custom-call | tf_op jit(solution)/shard_map/pallas_call | solution.py:426

commit v6 on v5

--- a/solution.py
+++ b/solution.py
@@ -327,21 +327,15 @@
     to_side(0).start()
     halo_wait(0, 3, 4)
     to_side(1).start()
+    merge(3, 0)
     halo_wait(1, 7, 4)
     steps(1, 6, 2, 4, 3, 2)
-    merge(3, 0)
-    merge(2, 1)
 
     @pl.loop(2, 8)
     def _(q):
-        @pl.when(q < 7)
-        def _():
-            halo_wait(q, 4 * q + 3, 4)
-
-        steps(4 * q - 1, 4, 4 * q - 2, 4, 4 * q - 3, 4)
-
         @pl.when(q == 2)
         def _():
+            merge(2, 1)
             merge(4, 0)
             merge(3, 1)
 
@@ -349,15 +343,21 @@
         def _():
             merge(5, 0)
             merge(4, 1)
+            merge(6, 0)
 
         @pl.when(q == 4)
         def _():
-            merge(6, 0)
             merge(5, 1)
 
         @pl.when(q == 5)
         def _():
             merge(6, 1)
+
+        @pl.when(q < 7)
+        def _():
+            halo_wait(q, 4 * q + 3, 4)
+
+        steps(4 * q - 1, 4, 4 * q - 2, 4, 4 * q - 3, 4)
 
     @pl.loop(0, 2)
     def _(t):

time: 42 us -> 40.2 us (0.957)
  Pallas kernels: 39.9 us -> 38.1 us
    pallas_call x1, Pallas kernels: 38.2 us -> 36.4 us  [shards(): pl.pallas_call(kernel, out_shape=tuple((pltpu.VMEM(s, f32) for s in shape...]
where the time goes in v6:
time: 40.2 us; the launch traced here: 40 us
  Pallas kernels  38.1 us (95%)
  between operations  1.93 us (5%)
    pallas_call x1, Pallas kernels, shards(): pl.pallas_call(kernel, out_shape=tuple((pltpu.VMEM(s, f32) for s in shape...  36.4 us
    pallas_call x1, Pallas kernels, shards(): pl.pallas_call(store, out_shape=tuple((jax.ShapeDtypeStruct(s, f32) for s...  1.68 us

profile of v6, /device:TPU:0, one launch (start us, length us, event | category | flops | bytes accessed | tf_op | source)
XLA Modules:
  0.0 40.0 jit_solution(1605401616071064919)
XLA Ops:
  1.9 36.4 %shard_map.77 = (f32[4,32,32,128]{3,2,1,0:T(8,128)S(1)}, f32[2,32,32,128]{3,2,1,0:T(8,128)S(1)}) custom-call(s32[1,1]{1,0:T(1,128)S(6)} %copy.8.leaving_in, s32[1,1]{1,0:T(1,128)S(6)} %copy.9.arriving_in, f32[2,4]{1,0:T(2,128)} %bitcast.2, f32[1,4]{1,0:T(1,128)} %bitcast.3, f32[4,32,32,128]{3,2,1,0:T(8,128)} %phases.1, f32[2,32,32,128]{3,2,1,0:T(8,128)} %potentials.1), custom_call_target="tpu_custom_call" | custom-call | flops 60000000 | bytes 6400000 | tf_op jit(solution)/shard_map/pallas_call | solution.py:405
  38.4 1.7 %shard_map.78 = (f32[4,32,32,128]{3,2,1,0:T(8,128)}, f32[2,32,32,128]{3,2,1,0:T(8,128)}) custom-call(f32[4,32,32,128]{3,2,1,0:T(8,128)S(1)} %get-tuple-element.4.phases, f32[2,32,32,128]{3,2,1,0:T(8,128)S(1)} %get-tuple-element.5.potentials), custom_call_target="tpu_custom_call" | custom-call | tf_op jit(solution)/shard_map/pallas_call | solution.py:426
